TPU v7x, 32 devices: a whole 2x2x4 slice. The times are simulated.
32 devices in a mesh: dp: 2 (over core), graph: 16 (over z, y, x).
Axes of the slice: x: 2, y: 2, z: 4, core: 2. Of those that a mesh axis runs over, the one named last changes fastest.
Arguments:
- node_latents: bfloat16 [8, 5120, 512], P('dp', 'graph'), may hold values from -6 to 6
- edge_latents: bfloat16 [8, 40960, 512], P('dp', 'graph'), may hold values from -6 to 6
- edge_first: bfloat16 [1536, 512], replicated, may hold values from -0.15625 to 0.15625
- edge_first_bias: float32 [512], replicated, may hold values from -3 to 3
- edge_second: bfloat16 [512, 512], replicated, may hold values from -0.25 to 0.25
- edge_second_bias: float32 [512], replicated, may hold values from -3 to 3
- edge_gain: float32 [512], replicated, may hold values from 0.5 to 1.5
- edge_shift: float32 [512], replicated, may hold values from -2 to 2
- node_first: bfloat16 [1024, 512], replicated, may hold values from -0.1875 to 0.1875
- node_first_bias: float32 [512], replicated, may hold values from -3 to 3
- node_second: bfloat16 [512, 512], replicated, may hold values from -0.25 to 0.25
- node_second_bias: float32 [512], replicated, may hold values from -3 to 3
- node_gain: float32 [512], replicated, may hold values from 0.5 to 1.5
- node_shift: float32 [512], replicated, may hold values from -2 to 2
- node_cot: bfloat16 [8, 5120, 512], P('dp', 'graph'), may hold values from -6 to 6
- edge_cot: bfloat16 [8, 40960, 512], P('dp', 'graph'), may hold values from -6 to 6
- send_index: int32 [16, 16, 12], P('graph'), may hold values from 0 to 317, as said below
- edge_sender: int32 [40960], P('graph'), may hold values from 0 to 511, as said below
- edge_receiver: int32 [40960], P('graph'), may hold values from 0 to 319, as said below
- node_mask: int32 [5120], P('graph'), may hold values from 0 to 1, as said below
Outputs:
- nodes_out: bfloat16 [8, 5120, 512], P('dp', 'graph')
- edges_out: bfloat16 [8, 40960, 512], P('dp', 'graph')
- node_grad: float32 [8, 5120, 512], P('dp', 'graph')
- edge_grad: bfloat16 [8, 40960, 512], P('dp', 'graph')
- edge_first_grad: float32 [1536, 512], replicated
- edge_first_bias_grad: float32 [512], replicated
- edge_second_grad: float32 [512, 512], replicated
- edge_second_bias_grad: float32 [512], replicated
- edge_gain_grad: float32 [512], replicated
- edge_shift_grad: float32 [512], replicated
- node_first_grad: float32 [1024, 512], replicated
- node_first_bias_grad: float32 [512], replicated
- node_second_grad: float32 [512, 512], replicated
- node_second_bias_grad: float32 [512], replicated
- node_gain_grad: float32 [512], replicated
- node_shift_grad: float32 [512], replicated
Inputs may be any that keep to these rules, and one draw needn't show every extreme that they name: `send_index`: each entry is a live node (mask 1) of the sending block, the first index. `edge_sender`: below 320: a live node of the edge's own block. Senders of edges with a padding receiver are arbitrary in range. `edge_receiver`: never decreases within a block's 2560 edges. An edge is live iff its receiver is live; the others come last in their block and point to node 319. Some block has all its edges live. `node_mask`: in each block of 320 nodes the live ones come first, at least half of them; the last 2 are padding.
All inputs are finite; a program needn't handle non-finite values.
Results may differ from a plain program's by a relative error of at most 0.0083.
Values may be sent and summed in bfloat16 or wider, within the bound.
No kernel may reach another device: no remote copies, remote signals or barrier semaphores. Data moves between devices by JAX's collectives and lax.ppermute only.
A program may use at most 320 MiB of HBM per device.

v0:
```python
import jax
import jax.numpy as jnp
from jax import lax
from jax.sharding import PartitionSpec as P

EPS = 1e-05


def from_behind(block, axis, distance):
    devices = range(lax.axis_size(axis))
    route = [((i - distance) % len(devices), i) for i in devices]
    return lax.ppermute(block, axis, route)


def project(row_values, weight):
    return jnp.einsum("snd,df->snf", row_values, weight, preferred_element_type=jnp.float32)


def project_back(row_grads, weight):
    return jnp.einsum("snf,df->snd", row_grads, weight, preferred_element_type=jnp.float32)


def outer_sum(row_values, row_grads):
    return jnp.einsum("snd,snf->df", row_values, row_grads, preferred_element_type=jnp.float32)


def normalize(pre_values):
    average = jnp.mean(pre_values, axis=-1, keepdims=True)
    centred = pre_values - average
    inverse = lax.rsqrt(jnp.mean(centred * centred, axis=-1, keepdims=True) + EPS)
    return (centred * inverse, inverse)


def norm_back(out_grad, normed, inverse, gain):
    scaled = out_grad * gain
    adjusted = scaled - jnp.mean(scaled, axis=-1, keepdims=True)
    adjusted = adjusted - normed * jnp.mean(scaled * normed, axis=-1, keepdims=True)
    return (adjusted * inverse).astype(jnp.bfloat16)


def silu_slope(hidden):
    logistic = jax.nn.sigmoid(hidden)
    return logistic * (1.0 + hidden * (1.0 - logistic))


def segment_rows(row_values, indices, segments):
    return jax.vmap(lambda slab: jax.ops.segment_sum(slab, indices, segments))(row_values)


def peer_offset(number, near):
    half = near // 2
    return number - half if number < half else number - half + 1


def shards(
    node_latents,
    edge_latents,
    edge_first,
    edge_first_bias,
    edge_second,
    edge_second_bias,
    edge_gain,
    edge_shift,
    node_first,
    node_first_bias,
    node_second,
    node_second_bias,
    node_gain,
    node_shift,
    node_cot,
    edge_cot,
    send_index,
    edge_sender,
    edge_receiver,
    node_mask,
):
    samples, nodes_here, width = node_latents.shape
    near = send_index.shape[1]
    slots = send_index.shape[2]
    table_rows = nodes_here + near * slots
    outgoing = send_index[0]
    node_live = node_mask.astype(jnp.float32)[None, :, None]
    edge_live = jnp.take(node_mask, edge_receiver).astype(jnp.float32)[None, :, None]
    w_edge = edge_first[:width]
    w_send = edge_first[width : 2 * width]
    w_recv = edge_first[2 * width :]
    arrived_parts = []
    for number in range(near):
        parcel = jnp.take(node_latents, outgoing[number], axis=1)
        arrived_parts.append(from_behind(parcel, "graph", peer_offset(number, near)))
    arrived = jnp.concatenate(arrived_parts, axis=1)
    row_table = jnp.concatenate([node_latents, arrived], axis=1)
    senders = jnp.take(row_table, edge_sender, axis=1)
    receivers = jnp.take(node_latents, edge_receiver, axis=1)
    edge_hidden = (
        project(edge_latents, w_edge)
        + project(senders, w_send)
        + project(receivers, w_recv)
        + edge_first_bias
    )
    edge_active = jax.nn.silu(edge_hidden).astype(jnp.bfloat16)
    edge_pre = project(edge_active, edge_second) + edge_second_bias
    edge_normed, edge_inverse = normalize(edge_pre)
    message = edge_live * (edge_normed * edge_gain + edge_shift)
    edges_out = (edge_latents.astype(jnp.float32) + message).astype(jnp.bfloat16)
    gathered = segment_rows(message, edge_receiver, nodes_here).astype(jnp.bfloat16)
    node_hidden = (
        project(node_latents, node_first[:width])
        + project(gathered, node_first[width:])
        + node_first_bias
    )
    node_active = jax.nn.silu(node_hidden).astype(jnp.bfloat16)
    node_pre = project(node_active, node_second) + node_second_bias
    node_normed, node_inverse = normalize(node_pre)
    nodes_out = (
        node_latents.astype(jnp.float32) + node_live * (node_normed * node_gain + node_shift)
    ).astype(jnp.bfloat16)
    node_up = node_cot.astype(jnp.float32)
    node_dq = node_live * node_up
    node_gain_grad = jnp.sum(node_dq * node_normed, axis=(0, 1))
    node_shift_grad = jnp.sum(node_dq, axis=(0, 1))
    node_pre_grad = norm_back(node_dq, node_normed, node_inverse, node_gain)
    node_second_bias_grad = jnp.sum(node_pre_grad.astype(jnp.float32), axis=(0, 1))
    node_second_grad = outer_sum(node_active, node_pre_grad)
    node_hidden_grad = (project_back(node_pre_grad, node_second) * silu_slope(node_hidden)).astype(
        jnp.bfloat16
    )
    node_first_bias_grad = jnp.sum(node_hidden_grad.astype(jnp.float32), axis=(0, 1))
    node_first_grad = jnp.concatenate(
        [outer_sum(node_latents, node_hidden_grad), outer_sum(gathered, node_hidden_grad)], axis=0
    )
    gathered_grad = project_back(node_hidden_grad, node_first[width:])
    node_grad = node_up + project_back(node_hidden_grad, node_first[:width])
    edge_up = edge_cot.astype(jnp.float32)
    message_grad = edge_live * (edge_up + jnp.take(gathered_grad, edge_receiver, axis=1))
    edge_gain_grad = jnp.sum(message_grad * edge_normed, axis=(0, 1))
    edge_shift_grad = jnp.sum(message_grad, axis=(0, 1))
    edge_pre_grad = norm_back(message_grad, edge_normed, edge_inverse, edge_gain)
    edge_second_bias_grad = jnp.sum(edge_pre_grad.astype(jnp.float32), axis=(0, 1))
    edge_second_grad = outer_sum(edge_active, edge_pre_grad)
    edge_hidden_grad = (project_back(edge_pre_grad, edge_second) * silu_slope(edge_hidden)).astype(
        jnp.bfloat16
    )
    edge_first_bias_grad = jnp.sum(edge_hidden_grad.astype(jnp.float32), axis=(0, 1))
    edge_grad = (edge_up + project_back(edge_hidden_grad, w_edge)).astype(jnp.bfloat16)
    w_edge_grad = outer_sum(edge_latents, edge_hidden_grad)
    w_send_grad = outer_sum(senders, edge_hidden_grad)
    w_recv_grad = outer_sum(receivers, edge_hidden_grad)
    node_grad = node_grad + segment_rows(
        project_back(edge_hidden_grad, w_recv), edge_receiver, nodes_here
    )
    table_grad = segment_rows(project_back(edge_hidden_grad, w_send), edge_sender, table_rows)
    outbound = table_grad[:, nodes_here:].reshape(samples, near, slots, width)
    returned_parts = []
    for number in range(near):
        returned_parts.append(
            from_behind(
                outbound[:, number].astype(jnp.bfloat16), "graph", -peer_offset(number, near)
            ).astype(jnp.float32)
        )
    returned = jnp.concatenate(returned_parts, axis=1)
    node_grad = (
        node_grad
        + table_grad[:, :nodes_here]
        + segment_rows(returned, outgoing.reshape(-1), nodes_here)
    )
    edge_first_grad = jnp.concatenate([w_edge_grad, w_send_grad, w_recv_grad], axis=0)
    totals = lax.psum(
        (
            edge_first_grad,
            edge_first_bias_grad,
            edge_second_grad,
            edge_second_bias_grad,
            edge_gain_grad,
            edge_shift_grad,
            node_first_grad,
            node_first_bias_grad,
            node_second_grad,
            node_second_bias_grad,
            node_gain_grad,
            node_shift_grad,
        ),
        ("dp", "graph"),
    )
    return (
        nodes_out,
        edges_out,
        node_grad,
        edge_grad,
        totals[0],
        totals[1],
        totals[2],
        totals[3],
        totals[4],
        totals[5],
        totals[6],
        totals[7],
        totals[8],
        totals[9],
        totals[10],
        totals[11],
    )


def solution(mesh):
    placed = (
        P("dp", "graph", None),
        P("dp", "graph", None),
        P(),
        P(),
        P(),
        P(),
        P(),
        P(),
        P(),
        P(),
        P(),
        P(),
        P(),
        P(),
        P("dp", "graph", None),
        P("dp", "graph", None),
        P("graph", None, None),
        P("graph"),
        P("graph"),
        P("graph"),
    )
    return jax.shard_map(
        shards,
        mesh=mesh,
        in_specs=placed,
        out_specs=(
            P("dp", "graph", None),
            P("dp", "graph", None),
            P("dp", "graph", None),
            P("dp", "graph", None),
            P(),
            P(),
            P(),
            P(),
            P(),
            P(),
            P(),
            P(),
            P(),
            P(),
            P(),
            P(),
        ),
        check_vma=False,
    )
```

profile of v0, /device:TPU:19, one launch (start us, length us, event | category | flops | bytes accessed | tf_op | source)
XLA Modules:
  0.0 1506.7 jit_solution(170203730770149168)
XLA Ops:
  47.2 36.3 %gather_fusion.2 = bf16[2560,4,512]{2,0,1:T(8,128)(2,1)} fusion(bf16[4,320,512]{2,1,0:T(8,128)(2,1)S(1)} %copy-done.3, s32[3072]{0:T(1024)S(1)} %pad_clamp_fusion.1), kind=kCustom, calls=%fused_computation.18 | custom fusion | bytes 20981760 | tf_op jit(solution)/shard_map/jit(_take)/gather | solution.py:94
  83.5 15.4 %gather_fusion = s32[2560]{0:T(1024)S(1)} fusion(s32[320]{0:T(512)S(1)} %copy-done.2, s32[3072]{0:T(1024)S(1)} %pad_clamp_fusion.1), kind=kCustom, calls=%fused_computation.16 | custom fusion | bytes 30720 | tf_op jit(solution)/shard_map/jit(_take)/gather | solution.py:83
  99.6 13.8 copy.75
  121.1 14.3 fusion.51
  145.4 13.7 copy.80
  159.2 14.1 copy.81
  197.9 12.8 gather_fusion.1
  210.8 16.9 %copy.73 = bf16[2560,4,512]{0,2,1:T(8,128)(2,1)} copy(bf16[2560,4,512]{2,1,0:T(4,128)(2,1)} %gather_fusion.1) | data formatting | bytes 20971520 | tf_op jit(solution)/shard_map/jit(_take)/gather | solution.py:93
  227.7 25.3 %multiply_convert_fusion.2 = (bf16[4,2560,512]{2,1,0:T(8,128)(2,1)S(1)}, f32[4,2560,512]{2,1,0:T(8,128)}) fusion(f32[512]{0:T(512)S(1)} %copy-done.73, f32[4,2560,512]{2,1,0:T(8,128)} %fusion.5, f32[4,2560,512]{2,1,0:T(8,128)} %fusion.51, bf16[1536,512]{1,0:T(8,128)(2,1)} %param.24, bf16[2560,4,512]{0,2,1:T(8,128)(2,1)} %copy.73, ...), kind=kOutput, calls=%fused_computation.37 | convolution fusion | flops 5415895040 | bytes 84414976 | tf_op jit(solution)/shard_map/snd,df->snf/dot_general | solution.py:16
  252.9 10.2 add_reduce_fusion
  263.2 10.5 multiply_reduce_fusion.2
  276.2 15.9 %add_convert_fusion = (bf16[4,2560,512]{1,2,0:T(8,128)(2,1)}, f32[2560,4,512]{0,2,1:T(8,128)}) fusion(bf16[4,2560,512]{1,2,0:T(8,128)(2,1)} %copy.80, f32[512]{0:T(512)S(1)} %copy-done.56, f32[512]{0:T(512)S(1)} %copy-done.42, f32[2560]{0:T(1024)S(1)} %copy-done.36, f32[4,2560]{1,0:T(4,128)S(1)} %add_rsqrt_fusion, ...), kind=kLoop, calls=%fused_computation.34 | loop fusion | flops 47185920 | bytes 63012864 | tf_op jit(solution)/shard_map/convert_element_type | solution.py:105
  292.1 24.6 %copy.78 = f32[2560,4,512]{2,1,0:T(4,128)} copy(f32[2560,4,512]{0,2,1:T(8,128)} %get-tuple-element.93) | data formatting | bytes 41943040 | tf_op jit(solution)/shard_map/mul | solution.py:104
  317.1 217.9 %scatter_fusion = f32[4,320,512]{2,0,1:T(4,128)S(1)} fusion(f32[4,320,512]{2,0,1:T(4,128)S(1)} %broadcast.104.clone, s32[2560]{0:T(1024)S(1)} %copy-done.31, f32[2560,4,512]{2,1,0:T(4,128)} %copy.78), kind=kCustom, calls=%fused_computation.20 | custom fusion | flops 5242880 | bytes 62924800 | tf_op jit(solution)/shard_map/vmap()/scatter-add | solution.py:47
  554.3 15.8 %gather_fusion.3 = f32[2560,4,512]{2,1,0:T(4,128)} fusion(f32[4,320,512]{2,0,1:T(4,128)S(1)} %copy.82, s32[3072]{0:T(1024)S(1)} %copy-done.34), kind=kCustom, calls=%fused_computation.19 | custom fusion | bytes 41953280 | tf_op jit(solution)/shard_map/jit(_take)/gather | solution.py:135
  570.1 24.0 %copy.83 = f32[2560,4,512]{0,2,1:T(8,128)} copy(f32[2560,4,512]{2,1,0:T(4,128)} %gather_fusion.3) | data formatting | bytes 41943040 | tf_op jit(solution)/shard_map/jit(_take)/gather | solution.py:135
  594.1 21.8 %multiply_reduce_fusion = (f32[512]{0:T(512)}, f32[4,2560]{1,0:T(4,128)S(1)}, f32[4,2560]{1,0:T(4,128)S(1)}, f32[512]{0:T(512)}, f32[4,2560,512]{1,2,0:T(8,128)S(1)}) fusion(f32[4,2560]{1,0:T(4,128)S(1)} %add_rsqrt_fusion, f32[4,2560]{1,0:T(4,128)S(1)} %broadcast_multiply_fusion.2, f32[4,2560,512]{1,2,0:T(8,128)} %get-tuple-element.114, ...), kind=kLoop, calls=%fused_computation.28 | loop fusion | flops 73378816 | bytes 73585152 | tf_op jit(solution)/shard_map/reduce_sum | solution.py:136
  615.9 15.9 %convert_reduce_fusion = (f32[512]{0:T(512)}, bf16[4,2560,512]{1,2,0:T(8,128)(2,1)}) fusion(f32[4,2560]{1,0:T(4,128)S(1)} %broadcast_multiply_fusion, f32[4,2560]{1,0:T(4,128)S(1)} %add_rsqrt_fusion, f32[4,2560]{1,0:T(4,128)S(1)} %broadcast_multiply_fusion.2, f32[4,2560,512]{1,2,0:T(8,128)} %get-tuple-element.114, f32[512]{0:T(512)S(1)} %copy-done.35, ...), kind=kLoop, calls=%fused_computation.29 | loop fusion | flops 57671168 | bytes 52598784 | tf_op jit(solution)/shard_map/reduce_sum | solution.py:139
  631.9 20.3 %convert_reduce_fusion.1 = (f32[512]{0:T(512)}, bf16[4,2560,512]{2,1,0:T(8,128)(2,1)}) fusion(f32[4,2560,512]{2,1,0:T(8,128)} %get-tuple-element.112, bf16[4,2560,512]{1,2,0:T(8,128)(2,1)} %get-tuple-element.88, bf16[512,512]{1,0:T(8,128)(2,1)S(1)} %copy-done), kind=kOutput, calls=%fused_computation.30 | convolution fusion | flops 5426380288 | bytes 42469376 | tf_op jit(solution)/shard_map/snf,df->snd/dot_general | solution.py:20
  652.1 12.2 fusion.29
  664.4 12.2 fusion.32
  686.1 12.3 convolution_bitcast_fusion.2
  709.4 31.8 %copy.85 = f32[2560,4,512]{2,1,0:T(4,128)} copy(f32[2560,4,512]{2,0,1:T(8,128)S(1)} %convolution_bitcast_fusion.1) | data formatting | bytes 41943040 | tf_op jit(solution)/shard_map/snf,df->snd/dot_general | solution.py:20
  743.8 324.7 %scatter_fusion.1 = f32[4,512,512]{2,0,1:T(4,128)} fusion(f32[4,512,512]{2,0,1:T(4,128)} %broadcast_in_dim.82, s32[2560]{0:T(1024)S(1)} %copy-done.38, f32[2560,4,512]{2,1,0:T(4,128)} %copy.85), kind=kCustom, calls=%fused_computation.21 | custom fusion | flops 5242880 | bytes 62924800 | tf_op jit(solution)/shard_map/vmap()/scatter-add | solution.py:47
  1072.4 12.6 fusion.1
  1104.0 13.5 convolution_bitcast_fusion
  1120.8 25.7 %copy.88 = f32[2560,4,512]{2,1,0:T(4,128)} copy(f32[2560,4,512]{2,0,1:T(8,128)} %convolution_bitcast_fusion) | data formatting | bytes 41943040 | tf_op jit(solution)/shard_map/snf,df->snd/dot_general | solution.py:20
  1146.5 13.8 copy.97
  1160.4 13.7 copy.95
  1174.2 217.7 %scatter_fusion.2 = f32[4,320,512]{2,0,1:T(4,128)S(1)} fusion(f32[4,320,512]{2,0,1:T(4,128)S(1)} %copy.87, s32[2560]{0:T(1024)S(1)} %copy-done.32, f32[2560,4,512]{2,1,0:T(4,128)} %copy.88), kind=kCustom, calls=%fused_computation.22 | custom fusion | flops 5242880 | bytes 62924800 | tf_op jit(solution)/shard_map/vmap()/scatter-add | solution.py:47
  1392.0 43.0 %all-reduce = (f32[512]{0:T(512)}, f32[512]{0:T(512)}, f32[512]{0:T(512)}, f32[512]{0:T(512)}, f32[512]{0:T(512)}, /*index=5*/f32[512]{0:T(512)}, f32[512]{0:T(512)}, f32[512]{0:T(512)}) all-reduce(f32[512]{0:T(512)S(1)} %copy-done.59, f32[512]{0:T(512)S(1)} %copy-done.52, ...), channel_id=1, replica_groups=mesh['dp'=2,'graph'=16] {'dp','graph'}, use_global_device_ids=true, to_apply=%region_14.16 | all-reduce | flops 4096 | bytes 32768 | tf_op jit(solution)/shard_map/psum | solution.py:168
  1460.9 25.2 %scatter_fusion.3 = f32[4,320,512]{2,0,1:T(4,128)} fusion(f32[4,320,512]{2,0,1:T(4,128)} %broadcast.104, s32[192]{0:T(256)S(1)} %copy-done.53, f32[192,4,512]{2,1,0:T(4,128)} %convert_bitcast_fusion), kind=kCustom, calls=%fused_computation.23 | custom fusion | flops 393216 | bytes 4719360 | tf_op jit(solution)/shard_map/vmap()/scatter-add | solution.py:47
  (385 shorter events, 193.0 us)
Async XLA Ops:
  7.2 1483.5 %all-reduce.4.cloned.1.call-start = ((), (), s32[]{:S(2)}) async-start(), calls=%async_computation | async-start | bytes 14680064 | tf_op jit(solution)/shard_map/psum | solution.py:168
  14.6 159.4 %collective-permute-start = (bf16[4,12,512]{2,1,0:T(8,128)(2,1)}, bf16[4,12,512]{2,1,0:T(8,128)(2,1)}, u32[]{:S(2)}, u32[]{:S(2)}) collective-permute-start(bf16[4,12,512]{2,1,0:T(8,128)(2,1)} %select_bitcast_fusion.15), channel_id=1, source_target_pairs={{8,0},{9,1},{10,2},{11,3},{12,4},{13,5},{14,6},{15,7},{0,8},{1,9},... | collective-permute-start | bytes 147464 | tf_op jit(solution)/shard_map/ppermute | solution.py:12
  17.0 159.8 %collective-permute-start.1 = (bf16[4,12,512]{2,1,0:T(8,128)(2,1)}, bf16[4,12,512]{2,1,0:T(8,128)(2,1)}, u32[]{:S(2)}, u32[]{:S(2)}) collective-permute-start(bf16[4,12,512]{2,1,0:T(8,128)(2,1)} %select_bitcast_fusion.14), channel_id=1, source_target_pairs={{7,0},{8,1},{9,2},{10,3},{11,4},{12,5},{13,6},{14,7},{15,8},{0,9},... | collective-permute-start | bytes 147464 | tf_op jit(solution)/shard_map/ppermute | solution.py:12
  22.5 155.7 %collective-permute-start.2 = (bf16[4,12,512]{2,1,0:T(8,128)(2,1)}, bf16[4,12,512]{2,1,0:T(8,128)(2,1)}, u32[]{:S(2)}, u32[]{:S(2)}) collective-permute-start(bf16[4,12,512]{2,1,0:T(8,128)(2,1)} %select_bitcast_fusion.13), channel_id=1, source_target_pairs={{6,0},{7,1},{8,2},{9,3},{10,4},{11,5},{12,6},{13,7},{14,8},{15,9},... | collective-permute-start | bytes 147464 | tf_op jit(solution)/shard_map/ppermute | solution.py:12
  25.0 154.4 %collective-permute-start.3 = (bf16[4,12,512]{2,1,0:T(8,128)(2,1)}, bf16[4,12,512]{2,1,0:T(8,128)(2,1)}, u32[]{:S(2)}, u32[]{:S(2)}) collective-permute-start(bf16[4,12,512]{2,1,0:T(8,128)(2,1)} %select_bitcast_fusion.12), channel_id=1, source_target_pairs={{5,0},{6,1},{7,2},{8,3},{9,4},{10,5},{11,6},{12,7},{13,8},{14,9},{... | collective-permute-start | bytes 147464 | tf_op jit(solution)/shard_map/ppermute | solution.py:12
  28.9 153.6 %collective-permute-start.4 = (bf16[4,12,512]{2,1,0:T(8,128)(2,1)}, bf16[4,12,512]{2,1,0:T(8,128)(2,1)}, u32[]{:S(2)}, u32[]{:S(2)}) collective-permute-start(bf16[4,12,512]{2,1,0:T(8,128)(2,1)} %select_bitcast_fusion.11), channel_id=1, source_target_pairs={{4,0},{5,1},{6,2},{7,3},{8,4},{9,5},{10,6},{11,7},{12,8},{13,9},{1... | collective-permute-start | bytes 147464 | tf_op jit(solution)/shard_map/ppermute | solution.py:12
  173.9 11.6 collective-permute-start.5
  176.8 8.9 collective-permute-start.6
  178.2 10.8 collective-permute-start.7
  179.4 11.7 collective-permute-start.8
  182.5 9.1 collective-permute-start.9
  185.6 8.2 collective-permute-start.10
  185.7 9.1 collective-permute-start.11
  189.0 5.9 collective-permute-start.12
  191.2 5.7 collective-permute-start.13
  191.6 6.0 collective-permute-start.14
  193.8 4.1 collective-permute-start.15
  1085.4 349.6 %collective-permute-start.16 = (bf16[4,12,512]{2,0,1:T(4,128)(2,1)S(1)}, bf16[4,12,512]{2,0,1:T(4,128)(2,1)}, u32[]{:S(2)}, u32[]{:S(2)}) collective-permute-start(bf16[4,12,512]{2,0,1:T(4,128)(2,1)S(1)} %get-tuple-element.110), channel_id=1, source_target_pairs={{8,0},{9,1},{10,2},{11,3},{12,4},{13,5},{14,6},{15,7},{0,8},{1,9},... | collective-permute-start | bytes 147464 | tf_op jit(solution)/shard_map/ppermute | solution.py:12
  1092.4 343.4 %collective-permute-start.17 = (bf16[4,12,512]{2,0,1:T(4,128)(2,1)S(1)}, bf16[4,12,512]{2,0,1:T(4,128)(2,1)}, u32[]{:S(2)}, u32[]{:S(2)}) collective-permute-start(bf16[4,12,512]{2,0,1:T(4,128)(2,1)S(1)} %get-tuple-element.109), channel_id=1, source_target_pairs={{9,0},{10,1},{11,2},{12,3},{13,4},{14,5},{15,6},{0,7},{1,8},{2,9},... | collective-permute-start | bytes 147464 | tf_op jit(solution)/shard_map/ppermute | solution.py:12
  1092.4 345.4 %collective-permute-start.18 = (bf16[4,12,512]{2,0,1:T(4,128)(2,1)S(1)}, bf16[4,12,512]{2,0,1:T(4,128)(2,1)}, u32[]{:S(2)}, u32[]{:S(2)}) collective-permute-start(bf16[4,12,512]{2,0,1:T(4,128)(2,1)S(1)} %get-tuple-element.108), channel_id=1, source_target_pairs={{10,0},{11,1},{12,2},{13,3},{14,4},{15,5},{0,6},{1,7},{2,8},{3,9},... | collective-permute-start | bytes 147464 | tf_op jit(solution)/shard_map/ppermute | solution.py:12
  1094.8 345.4 %collective-permute-start.19 = (bf16[4,12,512]{2,0,1:T(4,128)(2,1)S(1)}, bf16[4,12,512]{2,0,1:T(4,128)(2,1)S(1)}, u32[]{:S(2)}, u32[]{:S(2)}) collective-permute-start(bf16[4,12,512]{2,0,1:T(4,128)(2,1)S(1)} %get-tuple-element.107), channel_id=1, source_target_pairs={{11,0},{12,1},{13,2},{14,3},{15,4},{0,5},{1,6},{2,7},{3,8},{4,9},{... | collective-permute-start | bytes 147464 | tf_op jit(solution)/shard_map/ppermute | solution.py:12
  1100.4 339.9 %collective-permute-start.20 = (bf16[4,12,512]{2,0,1:T(4,128)(2,1)S(1)}, bf16[4,12,512]{2,0,1:T(4,128)(2,1)S(1)}, u32[]{:S(2)}, u32[]{:S(2)}) collective-permute-start(bf16[4,12,512]{2,0,1:T(4,128)(2,1)S(1)} %get-tuple-element.106), channel_id=1, source_target_pairs={{12,0},{13,1},{14,2},{15,3},{0,4},{1,5},{2,6},{3,7},{4,8},{5,9},{6... | collective-permute-start | bytes 147464 | tf_op jit(solution)/shard_map/ppermute | solution.py:12
  1435.0 7.5 collective-permute-start.21
  1435.8 10.0 collective-permute-start.22
  1437.8 10.2 collective-permute-start.23
  1440.3 7.8 collective-permute-start.24
  1440.4 8.1 collective-permute-start.25
  1442.4 11.1 collective-permute-start.26
  1445.8 7.8 collective-permute-start.27
  1448.0 5.7 collective-permute-start.28
  1448.1 5.7 collective-permute-start.29
  1448.4 7.5 collective-permute-start.30
  (81 other events, 2816.2 us)
Sparse Core Ops, SparseCore 0:
  1104.1 171.1 all-reduce.3
where the time goes:
time: 1530 us; the launch traced here: 1510 us
  other arithmetic  880 us (58%)
  local copies, waits for them, and re-layouts  332 us (22%)
  matrix products  176 us (12%)
  starting transfers between devices  53.8 us (4%)
  blocking collectives  43 us (3%)
  between operations  15.5 us (1%)
    scatter-add x4, other arithmetic, segment_rows(): jax.ops.segment_sum(slab, indices, segments)  786 us
    unnamed x201, local copies, waits for them, and re-layouts  81.5 us
    dot_general x7, matrix products, project(): jnp.einsum('snd,df->snf', row_values, weight, preferred_element_type=jnp....  64 us
    dot_general x7, matrix products, project_back(): jnp.einsum('snf,df->snd', row_grads, weight, preferred_element_type=jnp.f...  60 us
    dot_general x3, local copies, waits for them, and re-layouts, project_back(): jnp.einsum('snf,df->snd', row_grads, weight, preferred_element_type=jnp.f...  59.2 us
    ppermute x32, starting transfers between devices, from_behind(): return lax.ppermute(block, axis, route)  53.8 us
    dot_general x7, matrix products, outer_sum(): jnp.einsum('snd,snf->df', row_values, row_grads, preferred_element_type=j...  52 us
    gather x2, local copies, waits for them, and re-layouts, shards(): receivers = jnp.take(node_latents, edge_receiver, axis=1)  50 us
  transfers between devices with their start and end apart: 33, of which 5 were waited for; matrix products, arithmetic and copies ran while one was open for 32% of the time, Pallas kernels for 0%

commit v1 on v0

v1 whole, which is shorter than its diff:
```python
import functools

import jax
import jax.numpy as jnp
from jax import lax
from jax.experimental import pallas as pl
from jax.experimental.pallas import tpu as pltpu
from jax.sharding import PartitionSpec as P

EPS = 1e-05
VMEM = 60 * 1024 * 1024
BLOCK = 16
BATCH = 128
F32 = jnp.float32
BF16 = jnp.bfloat16


def dot(left, right):
    return jnp.dot(left, right, preferred_element_type=F32)


def dot_rows(left, right):
    return lax.dot_general(left, right, (((0,), (0,)), ((), ())), preferred_element_type=F32)


def dot_columns(left, right):
    return lax.dot_general(left, right, (((1,), (1,)), ((), ())), preferred_element_type=F32)


def fold(values):
    rows, width = values.shape
    return jnp.sum(values.reshape(rows // 8, 8, width), axis=0)


def logistic(values):
    return 0.5 * jnp.tanh(0.5 * values) + 0.5


def normalize(values):
    average = jnp.mean(values, axis=-1, keepdims=True)
    centred = values - average
    inverse = lax.rsqrt(jnp.mean(centred * centred, axis=-1, keepdims=True) + EPS)
    return centred * inverse, inverse


def norm_back(scaled, normed, inverse):
    average = jnp.mean(scaled, axis=-1, keepdims=True)
    along = jnp.mean(scaled * normed, axis=-1, keepdims=True)
    return inverse * (scaled - average - normed * along)


def lanes(values, width):
    return jnp.concatenate([values] * (width // values.shape[1]), axis=1)


def lane_parts(values):
    width = values.shape[1]
    return sum(values[:, at : at + 128] for at in range(128, width, 128)) + values[:, :128]


def row_sums(parts):
    return jnp.sum(jnp.concatenate(parts), axis=-1, keepdims=True)


def one_hot_columns(index_column, count):
    lanes = lax.broadcasted_iota(jnp.int32, (index_column.shape[0], count), 1).astype(F32)
    return jnp.where(index_column == lanes, 1.0, 0.0).astype(BF16)


def one_hot_rows(index_row, count):
    rows = lax.broadcasted_iota(jnp.int32, (count, index_row.shape[1]), 0).astype(F32)
    return jnp.where(index_row == rows, 1.0, 0.0).astype(BF16)


def edge_start(idx, x, nodes, first, vec, partial, inputs, table):
    tile, sample = pl.program_id(0), pl.program_id(1)
    width = x.shape[2]
    here = nodes.shape[1]

    @pl.when(tile == 0)
    def _():
        table[sample, :here] = (dot(nodes[sample], first[width : 2 * width]) * 0.5).astype(BF16)
        table[sample, here : 2 * here] = (
            (dot(nodes[sample], first[2 * width :]) + vec[0:1]) * 0.5
        ).astype(BF16)
        table[sample, 2 * here :] = first[:width] * 0.5

    @pl.when(sample == 0)
    def _():
        columns = idx[0].T
        inputs[:, :here] = one_hot_columns(columns[:, 0:1], here)
        inputs[:, here : 2 * here] = one_hot_columns(columns[:, 1:2], here)

    inputs[:, 2 * here :] = x[0]
    partial[0] = dot(inputs[...], table[sample]).astype(BF16)


def edge_forward(
    idx, count, partial, arrived, send, second, vec, node_vec,
    nodes_hbm, cot_hbm, node_first_hbm, node_second_hbm,
    act, bend, nrm, inv, vec_grad, nodes_out_hbm, base_hbm, gathered_grad_hbm, weight_grad_hbm,
    inputs, picks, table, live, degree, sums, node_inputs, node_actives, pre_grads, hidden_grads,
    projected, ordered, nodes, cot, node_first, node_second,
    nodes_out, base, gathered_grad, weight_grad, arrive, leave,
):
    tile, sample = pl.program_id(0), pl.program_id(1)
    samples, here, width = nodes.shape
    near = arrived.shape[0]
    slots = arrived.shape[1] // samples
    far = near * slots
    rows = partial.shape[1]
    chunk = rows // 4
    begin = (tile == 0) & (sample == 0)
    end = (tile == pl.num_programs(0) - 1) & (sample == samples - 1)
    incoming = [
        pltpu.make_async_copy(source, target, arrive.at[number])
        for number, (source, target) in enumerate(
            [
                (nodes_hbm, nodes),
                (cot_hbm, cot),
                (node_first_hbm, node_first),
                (node_second_hbm, node_second),
            ]
        )
    ]

    @pl.when(begin)
    def _():
        for copy in incoming:
            copy.start()
        foreign = arrived[...].reshape(samples * far, width)
        projected[...] = dot(foreign, send[...]) * 0.5
        sums[...] = jnp.zeros(sums.shape, F32)
        degree[...] = jnp.zeros(degree.shape, F32)
        table[...] = jnp.zeros(table.shape, BF16)
        for s in range(samples):
            for j in range(near):
                row = (j * samples + s) * slots
                ordered[j * slots : (j + 1) * slots] = projected[row : row + slots]
            table[s, :far] = ordered[...].astype(BF16)

    @pl.when(sample == 0)
    def _():
        columns = idx[0].T
        inputs[...] = one_hot_columns(columns[:, 0:1] - here, table.shape[1])
        live[...] = jnp.broadcast_to(columns[:, 2:3], live.shape)
        chosen = one_hot_rows(idx[0, 1:2], here)
        picks[...] = chosen
        counts = jnp.sum(chosen.astype(F32), axis=-1, keepdims=True)
        degree[...] += jnp.broadcast_to(counts, degree.shape)

    picked, pres = {}, {}

    def pick(number):
        at = slice(number * chunk, (number + 1) * chunk)
        picked[number] = dot(inputs[at], table[sample])

    def activate(number):
        for row in range(0, chunk, BLOCK):
            at = slice(number * chunk + row, number * chunk + row + BLOCK)
            value = partial[0, at].astype(F32) + picked[number][row : row + BLOCK]
            bent = jnp.tanh(value)
            twice = bent + 1.0
            silu = value * twice
            act[0, at] = silu.astype(BF16)
            bend[0, at] = (twice + silu * (1.0 - bent)).astype(BF16)
        pres[number] = dot(act[0, number * chunk : (number + 1) * chunk], second[...])

    def finish(number):
        for first_row in range(0, chunk, chunk // 2):
            batch = range(first_row, first_row + chunk // 2, BLOCK)
            values = [pres[number][row : row + BLOCK] + vec[1:2] for row in batch]
            average = row_sums([lane_parts(value) for value in values]) * (1.0 / width)
            centred = [
                value - average[n * BLOCK : (n + 1) * BLOCK] for n, value in enumerate(values)
            ]
            spread = row_sums([lane_parts(value * value) for value in centred]) * (1.0 / width)
            inverse = lax.rsqrt(spread + EPS)
            for n, row in enumerate(batch):
                at = slice(number * chunk + row, number * chunk + row + BLOCK)
                scale = inverse[n * BLOCK : (n + 1) * BLOCK] * live[at]
                nrm[0, at] = (centred[n] * lanes(scale, width)).astype(BF16)
                inv[0, at] = scale

    stages = (pick, activate, finish)
    for turn in range(4 + len(stages) - 1):
        for stage in reversed(range(len(stages))):
            if 0 <= turn - stage < 4:
                stages[stage](turn - stage)
    sums[sample] += dot(picks[...], nrm[0])

    @pl.when(end)
    def _():
        for copy in incoming:
            copy.wait()
        lines = lax.broadcasted_iota(jnp.int32, (here, 1), 0)
        alive = jnp.where(lines < count[0], 1.0, 0.0)
        shifts = lanes(degree[...], width) * vec[3:4]
        vectors = [jnp.zeros((8, width), F32) for _ in range(4)]
        hidden, pre, back = {}, {}, {}

        def first_layer(s):
            at = slice(s * here, (s + 1) * here)
            node_inputs[at, :width] = nodes[s]
            node_inputs[at, width:] = (sums[s] * vec[2:3] + shifts).astype(BF16)
            hidden[s] = dot(node_inputs[at], node_first[...])

        def second_layer(s):
            for row in range(0, here, BLOCK):
                at = slice(s * here + row, s * here + row + BLOCK)
                value = hidden[s][row : row + BLOCK] + node_vec[0:1]
                node_actives[at] = (value * logistic(value)).astype(BF16)
            pre[s] = dot(node_actives[s * here : (s + 1) * here], node_second[...])

        def norm(s):
            for row in range(0, here, BLOCK):
                inside = slice(row, row + BLOCK)
                normed, inverse = normalize(pre[s][inside] + node_vec[1:2])
                update = alive[inside] * (normed * node_vec[2:3] + node_vec[3:4])
                nodes_out[s, inside] = (nodes[s, inside].astype(F32) + update).astype(BF16)
                out_grad = alive[inside] * cot[s, inside].astype(F32)
                vectors[2] += fold(out_grad * normed)
                vectors[3] += fold(out_grad)
                pre_grad = norm_back(out_grad * node_vec[2:3], normed, inverse)
                vectors[1] += fold(pre_grad)
                pre_grads[s * here + row : s * here + row + BLOCK] = pre_grad.astype(BF16)
            pltpu.make_async_copy(nodes_out.at[s], nodes_out_hbm.at[s], leave.at[s]).start()
            back[s] = dot_columns(pre_grads[s * here : (s + 1) * here], node_second[...])

        def first_back(s):
            for row in range(0, here, BLOCK):
                at = slice(s * here + row, s * here + row + BLOCK)
                value = hidden[s][row : row + BLOCK] + node_vec[0:1]
                sigma = logistic(value)
                hidden_grad = back[s][row : row + BLOCK] * (sigma + value * sigma * (1.0 - sigma))
                vectors[0] += fold(hidden_grad)
                hidden_grads[at] = hidden_grad.astype(BF16)
            down = dot_columns(hidden_grads[s * here : (s + 1) * here], node_first[...])
            base[s] = cot[s].astype(F32) + down[:, :width]
            gathered_grad[s] = down[:, width:].astype(BF16)
            for number, (source, target) in enumerate(
                [(gathered_grad, gathered_grad_hbm), (base, base_hbm)]
            ):
                pltpu.make_async_copy(
                    source.at[s], target.at[s], leave.at[samples * (1 + number) + s]
                ).start()

        steps = (first_layer, second_layer, norm, first_back)
        for turn in range(samples + len(steps) - 1):
            for stage in reversed(range(len(steps))):
                if 0 <= turn - stage < samples:
                    steps[stage](turn - stage)
        weight_grad[: 2 * width] = dot_rows(node_inputs[...], hidden_grads[...]).astype(BF16)
        weight_grad[2 * width :] = dot_rows(node_actives[...], pre_grads[...]).astype(BF16)
        weights = pltpu.make_async_copy(weight_grad, weight_grad_hbm, leave.at[3 * samples])
        weights.start()
        for number in range(4):
            vec_grad[number] = vectors[number]
        for number, (source, target) in enumerate(
            [(nodes_out, nodes_out_hbm), (gathered_grad, gathered_grad_hbm), (base, base_hbm)]
        ):
            for s in range(samples):
                pltpu.make_async_copy(
                    source.at[s], target.at[s], leave.at[samples * number + s]
                ).wait()
        weights.wait()


def edge_backward(
    idx, early, late, cot, act, late_act, bend, nrm, inv, up, second, vec,
    x_hbm, act_hbm, send_hbm,
    hidden_out, vec_grad, local_hbm, remote_hbm, received_hbm, outbound_hbm, weight_grad_hbm,
    picks, narrow_picks, spread_a, spread_b, turned, pre_a, pre_b, hid_a, hid_b, dead_rows, flags,
    second_t, sums, first_grad, second_grad, ordered,
    final, final_act, send, local, remote, received, outbound, weight_grad, arrive, leave,
):
    step = pl.program_id(0)
    last = pl.num_programs(0) - 1
    samples, here, width = local.shape
    near = outbound.shape[0]
    slots = outbound.shape[1] // samples
    far = near * slots
    senders = here + far
    rows = early.shape[1]
    edges = x_hbm.shape[1]
    pairs = samples // 2
    window = narrow_picks.shape[1]
    pair = step % pairs
    before = 2 * (jnp.maximum(step - 1, 0) % pairs) + 1
    incoming = [
        pltpu.make_async_copy(source, target, arrive.at[number])
        for number, (source, target) in enumerate(
            [
                (x_hbm.at[samples - 1, pl.ds(edges - rows, rows)], final),
                (act_hbm.at[samples - 1, pl.ds(edges - rows, rows)], final_act),
                (send_hbm.at[pl.ds(width, width)], send),
            ]
        )
    ]

    @pl.when(step == 0)
    def _():
        for copy in incoming:
            copy.start()
        first_grad[...] = jnp.zeros(first_grad.shape, F32)
        second_grad[...] = jnp.zeros(second_grad.shape, F32)
        vec_grad[...] = jnp.zeros(vec_grad.shape, F32)
        sums[...] = jnp.zeros(sums.shape, F32)
        turned[width:] = jnp.ones((BLOCK, rows), BF16)
        pre_b[...] = jnp.zeros(pre_b.shape, BF16)
        hid_b[...] = jnp.zeros(hid_b.shape, BF16)
        spread_b[...] = jnp.zeros(spread_b.shape, BF16)
        second_t[...] = (second[...] * 0.5).T

    @pl.when(pair == 0)
    def _():
        receivers = idx[0, 1:2]
        lowest = jnp.min(jnp.where(receivers < 0.0, float(here), receivers)).astype(jnp.int32)
        highest = jnp.max(receivers).astype(jnp.int32)
        start = jnp.minimum(lowest // 16 * 16, here - window)
        flags[0] = (jnp.min(idx[0, 2:3]) < 0.5).astype(jnp.int32)
        flags[1] = (highest < start + window).astype(jnp.int32)
        flags[2] = start
        columns = idx[0].T[:, 1:2]
        picks[...] = one_hot_columns(columns, here)
        narrow_picks[...] = one_hot_columns(columns - start.astype(F32), window)
        dead_rows[...] = jnp.broadcast_to(1.0 - idx[0, 2:3], dead_rows.shape).astype(BF16)
        spread_a[:senders] = one_hot_rows(idx[0, 0:1], senders)
        spread_a[senders:] = one_hot_rows(idx[0, 1:2], here)

    @pl.when(pair == 1)
    def _():
        spread_b[...] = spread_a[...]

    def outer(act, pre):
        def piece(columns):
            if columns.start == 0:
                turned[:width] = act.T
            second_grad[:, columns] += dot(turned[...], pre[:, columns])

        return [lambda at=at: piece(at) for at in sides]

    def input_outer(x, hid):
        transposed = {}

        def piece(columns):
            if not transposed:
                transposed[0] = x.T
            first_grad[:, columns] += dot(transposed[0], hid[:, columns])

        return [lambda at=at: piece(at) for at in sides]

    def scatter(spread, hid, where):
        def piece(columns):
            sums[where, :, columns] += dot(spread[...], hid[:, columns])

        return [lambda at=at: piece(at) for at in sides]

    sides = [slice(0, width // 2), slice(width // 2, width)]

    def main(narrow):
        sums_at = [jnp.zeros((8, width), F32) for _ in range(2)]
        results = {}

        def norm_part(side, pre, first_row):
            batch = range(first_row, first_row + BATCH, BLOCK)
            kept, averages, slopes = [], [], []
            for row in batch:
                at = slice(row, row + BLOCK)
                normed = nrm[side, at].astype(F32)
                scaled = (cot[side, at].astype(F32) + results[side][at]) * vec[2:3]
                along = scaled * normed
                sums_at[0] += fold(along)
                sums_at[1] += fold(scaled)
                kept.append(scaled)
                averages.append(lane_parts(scaled))
                slopes.append(lane_parts(along))
            average = row_sums(averages) * (1.0 / width)
            slope = row_sums(slopes) * (1.0 / width)
            for n, row in enumerate(batch):
                at = slice(row, row + BLOCK)
                inside = slice(n * BLOCK, (n + 1) * BLOCK)
                change = kept[n] - average[inside] - slope[inside] * nrm[side, at].astype(F32)
                pre[at] = (change * lanes(inv[side, at], width)).astype(BF16)

        def silu_part(side, hid, first_row):
            for row in range(first_row, first_row + BATCH, BLOCK):
                at = slice(row, row + BLOCK)
                hidden_grad = (results[2 + side][at] * bend[side, at].astype(F32)).astype(BF16)
                hid[at] = hidden_grad
                hidden_out[side, at] = hidden_grad

        def interleave(part, pieces):
            batches = range(0, rows, BATCH)
            spots = [len(batches) * n // len(pieces) for n in range(len(pieces))]
            for number, row in enumerate(batches):
                while spots and number == spots[0]:
                    spots.pop(0)
                    pieces.pop(0)()
                part(row)

        def pick(side):
            if narrow:
                some = up[side, pl.ds(pl.multiple_of(flags[2], 16), window)]
                results[side] = dot(narrow_picks[...], some)
            else:
                results[side] = dot(picks[...], up[side])

        def back(side, pre):
            results[2 + side] = dot(pre[...], second_t[...])

        pick(0)
        interleave(
            lambda row: norm_part(0, pre_a, row),
            [lambda: pick(1)] + outer(late_act[0], pre_b),
        )
        interleave(
            lambda row: norm_part(1, pre_b, row),
            [lambda: back(0, pre_a)] + input_outer(late[0], hid_b),
        )
        interleave(
            lambda row: silu_part(0, hid_a, row),
            [lambda: back(1, pre_b)] + scatter(spread_b, hid_b, before),
        )
        interleave(
            lambda row: silu_part(1, hid_b, row),
            outer(act[0], pre_a)
            + input_outer(early[0], hid_a)
            + scatter(spread_a, hid_a, 2 * pair),
        )
        for number in range(2):
            vec_grad[2 + number] += sums_at[number]

    @pl.when(flags[1] == 1)
    def _():
        main(True)

    @pl.when(flags[1] == 0)
    def _():
        main(False)

    @pl.when(flags[0] == 1)
    def _():
        extra = dot(dead_rows[...], cot[0]) + dot(dead_rows[...], cot[1])
        vec_grad[3] -= extra[:8] * 0.125 * vec[2:3]

    @pl.when(step == last)
    def _():
        leaving = []

        def send_off(source, target):
            copy = pltpu.make_async_copy(source, target, leave.at[len(leaving)])
            copy.start()
            leaving.append(copy)

        def part(number):
            return pl.ds(number * width, width)

        for copy in incoming:
            copy.wait()
        for piece in outer(final_act[...], pre_b):
            piece()
        weight_grad[3 * width :] = second_grad[:width].astype(BF16)
        vec_grad[1] = second_grad[width : width + 8] * 0.125
        send_off(weight_grad.at[part(3)], weight_grad_hbm.at[part(3)])
        for piece in input_outer(final[...], hid_b) + scatter(spread_b, hid_b, samples - 1):
            piece()
        weight_grad[:width] = first_grad[...].astype(BF16)
        send_off(weight_grad.at[part(0)], weight_grad_hbm.at[part(0)])
        for s in range(samples):
            for j in range(near):
                row, place = here + j * slots, (j * samples + s) * slots
                ordered[place : place + slots] = sums[s, row : row + slots]
        remote[...] = ordered[...].astype(BF16)
        outbound[...] = dot_columns(remote[...], send[...]).astype(BF16).reshape(outbound.shape)
        send_off(outbound, outbound_hbm)
        send_off(remote, remote_hbm)
        local[...] = sums[:, :here].astype(BF16)
        send_off(local, local_hbm)
        received[...] = sums[:, senders:].astype(BF16)
        send_off(received, received_hbm)
        every = jnp.zeros((8, width), F32)
        for s in range(samples):
            every += fold(sums[s, :senders])
        vec_grad[0] = every
        for number in (2, 3):
            vec_grad[number] = vec_grad[number] / vec[2:3]
        for copy in leaving:
            copy.wait()


def edge_totals(
    local, received, remote, nodes, arrived, base, first, weights_in, after,
    node_grad, weights, made, leave,
):
    samples, here, width = nodes.shape
    owned = nodes[...].reshape(samples * here, width)
    mine = local[...].reshape(samples * here, width)
    got = received[...].reshape(samples * here, width)
    foreign = arrived[...].reshape(remote.shape)
    made[:width] = (dot_rows(owned, mine) + dot_rows(foreign, remote[...])).astype(BF16)
    made[width:] = dot_rows(owned, got).astype(BF16)
    copy = pltpu.make_async_copy(made, weights.at[pl.ds(width, 2 * width)], leave)
    copy.start()
    grads = dot_columns(mine, first[width : 2 * width]) + dot_columns(got, first[2 * width :])
    node_grad[...] = base[...] + grads.reshape(node_grad.shape)
    copy.wait()


def edge_outputs(idx, x_low, x_high, nrm_low, nrm_high, vec, after, edges_out, live):
    @pl.when(pl.program_id(1) == 0)
    def _():
        live[...] = jnp.broadcast_to(idx[0].T[:, 2:3], live.shape)

    rows = x_low.shape[1]
    for start, x, nrm in ((0, x_low, nrm_low), (rows, x_high, nrm_high)):
        for row in range(0, rows, BLOCK):
            inside = slice(row, row + BLOCK)
            at = slice(start + row, start + row + BLOCK)
            message = nrm[0, inside].astype(F32) * vec[2:3] + vec[3:4]
            message = jnp.where(lanes(live[at], message.shape[1]) > 0.0, message, 0.0)
            edges_out[0, at] = (x[0, inside].astype(F32) + message).astype(BF16)


def edge_gradient(cot_low, cot_high, hid_low, hid_high, first, after, edge_grad, first_t):
    @pl.when((pl.program_id(0) == 0) & (pl.program_id(1) == 0))
    def _():
        first_t[...] = first[...].T

    rows = cot_low.shape[1]
    for start, cot, hid in ((0, cot_low, hid_low), (rows, cot_high, hid_high)):
        at = slice(start, start + rows)
        edge_grad[0, at] = (cot[0].astype(F32) + dot(hid[0], first_t[...])).astype(BF16)


def unpack(totals, *refs):
    outs, (taken, given, arrive, leave) = refs[:-4], refs[-4:]
    rows = taken.shape[1]
    width = totals.shape[2]
    edge_half, node_half = 2 * width, (totals.shape[1] - 2 * width) // rows * rows
    places = []
    for core in range(2):
        for start, count, pair in ((0, edge_half, outs[:2]), (edge_half, node_half, outs[2:])):
            for row in range(0, count, rows):
                goal = core * count + row
                if goal < pair[0].shape[0]:
                    places.append((core, start + row, pair[0], goal))
                else:
                    places.append((core, start + row, pair[1], goal - pair[0].shape[0]))
    incoming = [
        pltpu.make_async_copy(totals.at[core, pl.ds(row, rows)], taken.at[n], arrive.at[n])
        for n, (core, row, _, _) in enumerate(places)
    ]
    leaving = [
        pltpu.make_async_copy(given.at[n], goal.at[pl.ds(row, rows)], leave.at[n])
        for n, (_, _, goal, row) in enumerate(places)
    ]
    for copy in incoming:
        copy.start()
    for n in range(len(places)):
        incoming[n].wait()
        given[n] = taken[n].astype(F32)
        leaving[n].start()
    for copy in leaving:
        copy.wait()


def whole(shape):
    return pl.BlockSpec(
        shape, lambda *_: (0,) * len(shape), pipeline_mode=pl.Buffered(buffer_count=1)
    )


def unread():
    return pl.BlockSpec(memory_space=pl.ANY)


def params(steps):
    return pltpu.CompilerParams(
        dimension_semantics=("arbitrary",) * steps, vmem_limit_bytes=VMEM
    )


def peer_offset(number, near):
    half = near // 2
    return number - half if number < half else number - half + 1


def shift(block, distance):
    size = lax.axis_size("graph")
    return lax.ppermute(block, "graph", [(i, (i + distance) % size) for i in range(size)])


def all_peers(near):
    return lax.axis_size("graph") == near


def exchange(chunks, sign):
    near = chunks.shape[0]
    if not all_peers(near):
        return jnp.stack([shift(chunks[j], sign * peer_offset(j, near)) for j in range(near)])
    me = lax.axis_index("graph")
    swapped = lax.all_to_all(chunks, "graph", 0, 0)
    own = lax.dynamic_index_in_dim(chunks, me, 0, keepdims=False)
    opposite = shift(own, near // 2)
    mine = (jnp.arange(near) == me)[:, None, None]
    return jnp.where(mine, opposite[None], swapped)


def chunk_order(send_index):
    near = send_index.shape[0]
    if not all_peers(near):
        return send_index
    numbers = jnp.arange(near, dtype=jnp.int32)
    distance = (numbers - lax.axis_index("graph") + near) % near
    number = jnp.where(distance <= near // 2, distance + near // 2 - 1, distance - near // 2)
    number = jnp.where(distance == 0, 0, number)
    chosen = number[:, None, None] == numbers[None, :, None]
    return jnp.sum(jnp.where(chosen, send_index[None], 0), axis=1)


def chunk_rows(edge_sender, here, near, slots):
    if not all_peers(near):
        return edge_sender
    slot = edge_sender - here
    number = slot // slots
    offset = number - near // 2 + (number >= near // 2).astype(jnp.int32)
    offset = jnp.where(number == 0, 0, offset)
    owner = (lax.axis_index("graph") - offset + near) % near
    return jnp.where(slot < 0, edge_sender, here + owner * slots + slot % slots)


def rounded(values):
    return lax.reduce_precision(values, 8, 7)


def split_rows(vectors):
    high = rounded(vectors)
    return jnp.concatenate([high, rounded(vectors - high)])


def repeat(block, count):
    return jnp.broadcast_to(block[None], (count,) + block.shape)


def scatter_all(grads):
    rows, width = grads.shape
    parts = 2 * lax.axis_size("graph")
    return lax.all_to_all(grads.reshape(parts, rows // parts, width), ("dp", "graph"), 0, 0)


def add_parts(parts):
    return jnp.sum(parts.astype(F32), axis=0)


def side_groups():
    size = lax.axis_size("graph")
    return [list(range(size // 2)), list(range(size // 2, size))]


def swap_sides(block):
    return shift(block, lax.axis_size("graph") // 2)


def both_sides(piece, other):
    size = lax.axis_size("graph")
    low = lax.axis_index("graph") < size // 2
    return jnp.concatenate([jnp.where(low, piece, other), jnp.where(low, other, piece)])


def exchange_in_side(pieces):
    return lax.all_to_all(pieces, "graph", 0, 0, axis_index_groups=side_groups())


def gather_cores(block):
    return lax.all_to_all(repeat(block, 2), "dp", 0, 0)


def pair_pieces(grads, vectors):
    rows, width = grads.shape
    size = lax.axis_size("graph") // 2
    half = rows // 2
    core = lax.axis_index("dp")
    leaving = lax.dynamic_slice_in_dim(grads, (1 - core) * half, half)
    other = lax.ppermute(leaving, "dp", [(0, 1), (1, 0)])
    mine = lax.dynamic_slice_in_dim(grads, core * half, half)
    pieces = (mine.astype(F32) + other.astype(F32)).astype(BF16)
    pieces = pieces.reshape(size, half // size, width)
    return jnp.concatenate([pieces, repeat(split_rows(vectors).astype(BF16), size)], axis=1)


def shards(
    node_latents,
    edge_latents,
    edge_first,
    edge_first_bias,
    edge_second,
    edge_second_bias,
    edge_gain,
    edge_shift,
    node_first,
    node_first_bias,
    node_second,
    node_second_bias,
    node_gain,
    node_shift,
    node_cot,
    edge_cot,
    send_index,
    edge_sender,
    edge_receiver,
    node_mask,
):
    samples, here, width = node_latents.shape
    edges = edge_latents.shape[1]
    near, slots = send_index.shape[1:]
    far = near * slots
    senders = here + far

    targets = chunk_order(send_index[0])
    targets = targets[:, None, :] + here * jnp.arange(samples, dtype=jnp.int32)[None, :, None]
    pick = jax.nn.one_hot(targets.reshape(-1), samples * here, dtype=BF16)
    parcels = dot(pick, node_latents.reshape(samples * here, width)).astype(BF16)
    arrived = exchange(parcels.reshape(near, samples * slots, width), 1)

    edge_live = edge_receiver < here - 1
    idx = jnp.stack(
        [
            chunk_rows(edge_sender, here, near, slots).astype(F32),
            jnp.where(edge_live, edge_receiver, -1).astype(F32),
            edge_live.astype(F32),
        ]
    )
    idx = jnp.pad(idx, ((0, 5), (0, 0)))
    zero = jnp.zeros((width,), F32)
    edge_vec = jnp.stack(
        [edge_first_bias, edge_second_bias, edge_gain, edge_shift, zero, zero, zero, zero]
    )
    node_vec = jnp.stack(
        [node_first_bias, node_second_bias, node_gain, node_shift, zero, zero, zero, zero]
    )
    unit = 2 * samples * edges * width * width

    def third(number):
        return pl.BlockSpec(
            (width, width), lambda *_: (number, 0), pipeline_mode=pl.Buffered(buffer_count=1)
        )

    edge_shape = jax.ShapeDtypeStruct((samples, edges, width), BF16)
    inv_shape = jax.ShapeDtypeStruct((samples, edges, 128), F32)
    node_shape = jax.ShapeDtypeStruct((samples, here, width), BF16)
    node_sums_shape = jax.ShapeDtypeStruct((samples, here, width), F32)
    vec_shape = jax.ShapeDtypeStruct((4, 8, width), F32)

    def edge_block(rows):
        return pl.BlockSpec((1, rows, width), lambda t, s: (s, t, 0))

    def two_halves(rows):
        return [
            pl.BlockSpec((1, rows // 2, width), lambda t, s, n=n: (s, 2 * t + n, 0))
            for n in range(2)
        ]

    def idx_block(rows):
        return pl.BlockSpec((1, 8, rows), lambda t, s: (t, 0, 0))

    def inv_block(rows):
        return pl.BlockSpec((1, rows, 128), lambda t, s: (s, t, 0))

    def tiled(rows):
        return idx.reshape(8, edges // rows, rows).transpose(1, 0, 2)

    wide = edges // 2
    partial = pl.pallas_call(
        edge_start,
        grid=(edges // wide, samples),
        in_specs=[
            idx_block(wide),
            edge_block(wide),
            whole((samples, here, width)),
            whole((3 * width, width)),
            whole((8, width)),
        ],
        out_specs=edge_block(wide),
        out_shape=edge_shape,
        scratch_shapes=[
            pltpu.VMEM((wide, 2 * here + width), BF16),
            pltpu.VMEM((samples, 2 * here + width, width), BF16),
        ],
        compiler_params=params(2),
        cost_estimate=pl.CostEstimate(
            flops=3 * unit, bytes_accessed=4 * samples * edges * width, transcendentals=0
        ),
        name="edge_start",
    )(tiled(wide), edge_latents, node_latents, edge_first, edge_vec)

    count = jnp.sum(node_mask).reshape(1)
    remote = -(-far // 128) * 128
    (
        act, bend, nrm, inv, node_sums, nodes_out, base, gathered_grad, node_weights
    ) = pl.pallas_call(
        edge_forward,
        grid=(edges // wide, samples),
        in_specs=[
            idx_block(wide),
            pl.BlockSpec(memory_space=pltpu.SMEM),
            edge_block(wide),
            whole((near, samples * slots, width)),
            third(1),
            whole((width, width)),
            whole((8, width)),
            whole((8, width)),
        ]
        + [unread()] * 4,
        out_specs=[edge_block(wide)] * 3
        + [inv_block(wide), whole((4, 8, width))]
        + [unread()] * 4,
        out_shape=[
            edge_shape,
            edge_shape,
            edge_shape,
            inv_shape,
            vec_shape,
            node_shape,
            node_sums_shape,
            node_shape,
            jax.ShapeDtypeStruct((3 * width, width), BF16),
        ],
        scratch_shapes=[
            pltpu.VMEM((wide, remote), BF16),
            pltpu.VMEM((here, wide), BF16),
            pltpu.VMEM((samples, remote, width), BF16),
            pltpu.VMEM((wide, 128), F32),
            pltpu.VMEM((here, 128), F32),
            pltpu.VMEM((samples, here, width), F32),
            pltpu.VMEM((samples * here, 2 * width), BF16),
            pltpu.VMEM((samples * here, width), BF16),
            pltpu.VMEM((samples * here, width), BF16),
            pltpu.VMEM((samples * here, width), BF16),
            pltpu.VMEM((samples * far, width), F32),
            pltpu.VMEM((far, width), F32),
            pltpu.VMEM((samples, here, width), BF16),
            pltpu.VMEM((samples, here, width), BF16),
            pltpu.VMEM((2 * width, width), BF16),
            pltpu.VMEM((width, width), BF16),
            pltpu.VMEM((samples, here, width), BF16),
            pltpu.VMEM((samples, here, width), F32),
            pltpu.VMEM((samples, here, width), BF16),
            pltpu.VMEM((3 * width, width), BF16),
            pltpu.SemaphoreType.DMA((4,)),
            pltpu.SemaphoreType.DMA((3 * samples + 1,)),
        ],
        compiler_params=params(2),
        cost_estimate=pl.CostEstimate(
            flops=4 * unit, bytes_accessed=8 * samples * edges * width, transcendentals=0
        ),
        name="edge_forward",
    )(
        tiled(wide), count, partial, arrived, edge_first, edge_second, edge_vec, node_vec,
        node_latents, node_cot, node_first, node_second,
    )
    node_parts = scatter_all(node_weights)

    short = edges // 5
    pairs = samples // 2

    def paired(lanes_here):
        return pl.BlockSpec((2, short, lanes_here), lambda i: (i % pairs, i // pairs, 0))

    def early_half(i):
        return (2 * (i % pairs), i // pairs, 0)

    def late_half(i):
        j = jnp.maximum(i - 1, 0)
        return (2 * (j % pairs) + 1, j // pairs, 0)

    (
        hidden_grad, edge_sums, local, remote_sums, received, outbound, edge_weights
    ) = pl.pallas_call(
        edge_backward,
        grid=(edges // short * pairs,),
        in_specs=[
            pl.BlockSpec((1, 8, short), lambda i: (i // pairs, 0, 0)),
            pl.BlockSpec((1, short, width), early_half),
            pl.BlockSpec((1, short, width), late_half),
            paired(width),
            pl.BlockSpec((1, short, width), early_half),
            pl.BlockSpec((1, short, width), late_half),
            paired(width),
            paired(width),
            paired(128),
            pl.BlockSpec((2, here, width), lambda i: (i % pairs, 0, 0)),
            whole((width, width)),
            whole((8, width)),
        ]
        + [unread()] * 3,
        out_specs=[paired(width), whole((4, 8, width))] + [unread()] * 5,
        out_shape=[
            edge_shape,
            vec_shape,
            node_shape,
            jax.ShapeDtypeStruct((samples * far, width), BF16),
            node_shape,
            jax.ShapeDtypeStruct((near, samples * slots, width), BF16),
            jax.ShapeDtypeStruct((4 * width, width), BF16),
        ],
        scratch_shapes=[
            pltpu.VMEM((short, here), BF16),
            pltpu.VMEM((short, min(256, here)), BF16),
            pltpu.VMEM((senders + here, short), BF16),
            pltpu.VMEM((senders + here, short), BF16),
            pltpu.VMEM((width + BLOCK, short), BF16),
            pltpu.VMEM((short, width), BF16),
            pltpu.VMEM((short, width), BF16),
            pltpu.VMEM((short, width), BF16),
            pltpu.VMEM((short, width), BF16),
            pltpu.VMEM((BLOCK, short), BF16),
            pltpu.SMEM((3,), jnp.int32),
            pltpu.VMEM((width, width), BF16),
            pltpu.VMEM((samples, senders + here, width), F32),
            pltpu.VMEM((width, width), F32),
            pltpu.VMEM((width + BLOCK, width), F32),
            pltpu.VMEM((samples * far, width), F32),
            pltpu.VMEM((short, width), BF16),
            pltpu.VMEM((short, width), BF16),
            pltpu.VMEM((width, width), BF16),
            pltpu.VMEM((samples, here, width), BF16),
            pltpu.VMEM((samples * far, width), BF16),
            pltpu.VMEM((samples, here, width), BF16),
            pltpu.VMEM((near, samples * slots, width), BF16),
            pltpu.VMEM((4 * width, width), BF16),
            pltpu.SemaphoreType.DMA((3,)),
            pltpu.SemaphoreType.DMA((6,)),
        ],
        compiler_params=params(1),
        cost_estimate=pl.CostEstimate(
            flops=7 * unit, bytes_accessed=10 * samples * edges * width, transcendentals=0
        ),
        name="edge_backward",
    )(
        tiled(short), edge_latents, edge_latents, edge_cot, act, act, bend, nrm, inv,
        gathered_grad, edge_second, edge_vec,
        edge_latents, act, edge_first,
    )
    node_parts, edge_weights, outbound = lax.optimization_barrier(
        (node_parts, edge_weights, outbound)
    )
    returned = exchange(outbound, -1)
    node_partial, edge_weights = pl.pallas_call(
        edge_totals,
        in_specs=[
            whole((samples, here, width)),
            whole((samples, here, width)),
            whole((samples * far, width)),
            whole((samples, here, width)),
            whole((near, samples * slots, width)),
            whole((samples, here, width)),
            whole((3 * width, width)),
            unread(),
            unread(),
        ],
        out_specs=[whole((samples, here, width)), unread()],
        out_shape=[node_sums_shape, jax.ShapeDtypeStruct((4 * width, width), BF16)],
        input_output_aliases={7: 1},
        scratch_shapes=[pltpu.VMEM((2 * width, width), BF16), pltpu.SemaphoreType.DMA],
        compiler_params=pltpu.CompilerParams(vmem_limit_bytes=VMEM),
        name="edge_totals",
    )(
        local, received, remote_sums, node_latents, arrived, base, edge_first, edge_weights,
        outbound,
    )
    vectors = jnp.concatenate([edge_sums, node_sums]).sum(axis=1)
    count = vectors.shape[0]
    pieces = pair_pieces(edge_weights, vectors)
    node_piece = add_parts(node_parts).astype(BF16)
    pieces, returned, node_piece = lax.optimization_barrier((pieces, returned, node_piece))
    arrived_pieces = exchange_in_side(pieces)
    edge_grad = pl.pallas_call(
        edge_gradient,
        grid=(edges // wide, samples),
        in_specs=[*two_halves(wide), *two_halves(wide), third(0), unread()],
        out_specs=edge_block(wide),
        out_shape=edge_shape,
        scratch_shapes=[pltpu.VMEM((width, width), BF16)],
        compiler_params=params(2),
        cost_estimate=pl.CostEstimate(
            flops=unit, bytes_accessed=6 * samples * edges * width, transcendentals=0
        ),
        name="edge_gradient",
    )(edge_cot, edge_cot, hidden_grad, hidden_grad, edge_first, pieces)
    arrived_pieces, edge_grad = lax.optimization_barrier((arrived_pieces, edge_grad))
    partial_sums = add_parts(arrived_pieces)
    piece = partial_sums.shape[0] - 2 * count
    vectors = split_rows(partial_sums[piece : piece + count] + partial_sums[piece + count :])
    partial_sums = jnp.concatenate([rounded(partial_sums[:piece]), vectors])
    other = swap_sides(jnp.concatenate([partial_sums.astype(BF16), node_piece]))
    totals = partial_sums + other[: piece + 2 * count].astype(F32)
    node_pair = both_sides(node_piece, other[piece + 2 * count :])
    vectors = totals[piece : piece + count] + totals[piece + count :]
    joined = jnp.concatenate([totals[:piece].astype(BF16), node_pair])
    gathered_rows = exchange_in_side(repeat(joined, lax.axis_size("graph") // 2))
    edges_out = pl.pallas_call(
        edge_outputs,
        grid=(edges // wide, samples),
        in_specs=[
            idx_block(wide),
            *two_halves(wide),
            *two_halves(wide),
            whole((8, width)),
            unread(),
        ],
        out_specs=edge_block(wide),
        out_shape=edge_shape,
        scratch_shapes=[pltpu.VMEM((wide, 128), F32)],
        compiler_params=params(2),
        cost_estimate=pl.CostEstimate(
            flops=0, bytes_accessed=6 * samples * edges * width, transcendentals=0
        ),
        name="edge_outputs",
    )(
        tiled(wide), edge_latents, edge_latents, nrm, nrm, edge_vec, joined,
    )
    gathered_rows, edges_out = lax.optimization_barrier((gathered_rows, edges_out))
    nodes_rows = gathered_rows[:, piece:]
    nodes_rows = nodes_rows.reshape(nodes_rows.shape[0], 2, -1, width).transpose(1, 0, 2, 3)
    halves = [
        gathered_rows[:, :piece].reshape(2 * width, width),
        nodes_rows.reshape(-1, width),
    ]
    totals = gather_cores(jnp.concatenate(halves + [split_rows(vectors).astype(BF16)]))
    chunk = width // 2
    parts = 7 * width // chunk
    weights = pl.pallas_call(
        unpack,
        in_specs=[unread()],
        out_specs=[unread()] * 4,
        out_shape=[
            jax.ShapeDtypeStruct((rows * width, width), F32) for rows in (3, 1, 2, 1)
        ],
        scratch_shapes=[
            pltpu.VMEM((parts, chunk, width), BF16),
            pltpu.VMEM((parts, chunk, width), F32),
            pltpu.SemaphoreType.DMA((parts,)),
            pltpu.SemaphoreType.DMA((parts,)),
        ],
        compiler_params=pltpu.CompilerParams(vmem_limit_bytes=VMEM),
        name="unpack",
    )(totals)
    vectors = totals[:, -2 * count :].astype(F32).sum(axis=0)
    vectors = vectors[:count] + vectors[count:]

    node_grad = node_partial + dot_rows(pick, returned.reshape(-1, width)).reshape(
        samples, here, width
    )
    return (
        nodes_out,
        edges_out,
        node_grad,
        edge_grad,
        weights[0],
        vectors[0],
        weights[1],
        vectors[1],
        vectors[2],
        vectors[3],
        weights[2],
        vectors[4],
        weights[3],
        vectors[5],
        vectors[6],
        vectors[7],
    )


def solution(mesh):
    rows = P("dp", "graph", None)
    placed = (rows, rows) + (P(),) * 12 + (rows, rows)
    placed += (P("graph", None, None), P("graph"), P("graph"), P("graph"))
    return jax.shard_map(
        shards,
        mesh=mesh,
        in_specs=placed,
        out_specs=(rows,) * 4 + (P(),) * 12,
        check_vma=False,
    )
```

time: 1530 us -> 237 us (0.15); the launches traced: 1510 us -> 236 us
  other arithmetic: 880 us -> 9.76 us
  local copies, waits for them, and re-layouts: 332 us -> 10.4 us
  matrix products: 176 us -> 4.68 us
  Pallas kernels: 0 us -> 152 us
  blocking collectives: 43 us -> 7.93 us
  starting transfers between devices: 53.8 us -> 35.6 us
    scatter-add x4 -> x0, other arithmetic: 786 us -> none  [segment_rows(): jax.ops.segment_sum(slab, indices, segments)]
    dot_general x21 -> x2, matrix products: 176 us -> 4.68 us  [the longest x1 3.45 us: dot(): return jnp.dot(left, right, preferred_element_type=F32)]
    pallas_call x0 -> x7, Pallas kernels: none -> 152 us  [the longest x1 49 us: shards(): pl.pallas_call(edge_backward, grid=(edges // short * pairs,), in_specs=[p...]
    gather x23 -> x0, local copies, waits for them, and re-layouts: 150 us -> none  [the longest x2 50 us: shards(): receivers = jnp.take(node_latents, edge_receiver, axis=1)]
    unnamed x201 -> x37, local copies, waits for them, and re-layouts: 81.5 us -> 2.36 us
    dot_general x3 -> x0, local copies, waits for them, and re-layouts: 59.2 us -> none  [project_back(): jnp.einsum('snf,df->snd', row_grads, weight, preferred_element_type=jnp.f...]
    ppermute x32 -> x4, starting transfers between devices: 53.8 us -> 2.23 us  [the longest x3 1.3 us: shift(): lax.ppermute(block, 'graph', [(i, (i + distance) % size) for i in range(s...]
    reduce_sum x6, other arithmetic: 54.2 us -> 2.76 us  [the longest x2 1.8 us: add_parts(): return jnp.sum(parts.astype(F32), axis=0)]
  transfers between devices with their start and end apart: 33 -> 9, of which waited for: 5 -> 4; matrix products, arithmetic and copies ran while one was open for 32% -> 6% of each run, Pallas kernels for 0% -> 47%
where the time goes in v1:
time: 237 us; the launch traced here: 236 us
  Pallas kernels  152 us (64%)
  starting transfers between devices  35.6 us (15%)
  waiting for transfers between devices  14.4 us (6%)
  local copies, waits for them, and re-layouts  10.4 us (4%)
  other arithmetic  9.76 us (4%)
  blocking collectives  7.93 us (3%)
  matrix products  4.68 us (2%)
    pallas_call x1, Pallas kernels, shards(): pl.pallas_call(edge_backward, grid=(edges // short * pairs,), in_specs=[p...  49 us
    pallas_call x1, Pallas kernels, shards(): pl.pallas_call(edge_forward, grid=(edges // wide, samples), in_specs=[idx...  37.2 us
    pallas_call x1, Pallas kernels, shards(): pl.pallas_call(edge_start, grid=(edges // wide, samples), in_specs=[idx_b...  22.6 us
    pallas_call x1, Pallas kernels, shards(): pl.pallas_call(edge_gradient, grid=(edges // wide, samples), in_specs=[*t...  15.5 us
    pallas_call x1, Pallas kernels, shards(): pl.pallas_call(edge_outputs, grid=(edges // wide, samples), in_specs=[idx...  15 us
    all_to_all x2, starting transfers between devices, exchange(): swapped = lax.all_to_all(chunks, 'graph', 0, 0)  13.5 us
    all_to_all x2, starting transfers between devices, exchange_in_side(): lax.all_to_all(pieces, 'graph', 0, 0, axis_index_groups=side_groups())  13 us
    ppermute x3, waiting for transfers between devices, shift(): lax.ppermute(block, 'graph', [(i, (i + distance) % size) for i in range(s...  9.06 us
  transfers between devices with their start and end apart: 9, of which 4 were waited for; matrix products, arithmetic and copies ran while one was open for 6% of the time, Pallas kernels for 47%

profile of v1, /device:TPU:19, one launch (start us, length us, event | category | flops | bytes accessed | tf_op | source)
XLA Modules:
  0.0 236.2 jit_solution(5934017321179449117)
XLA Ops:
  2.1 3.4 %fusion.6 = bf16[768,512]{1,0:T(8,128)(2,1)} fusion(bf16[1280,512]{1,0:T(8,128)(2,1)} %bitcast.49, s32[768]{0:T(1024)S(1)} %add.126), kind=kOutput, calls=%fused_computation.10 | convolution fusion | flops 1008009216 | bytes 2100224 | tf_op jit(solution)/shard_map/dot_general | solution.py:19
  5.5 6.5 %all-to-all-start = ((bf16[16,48,512]{2,1,0:T(8,128)(2,1)}), bf16[16,48,512]{2,1,0:T(8,128)(2,1)S(1)}, u32[]{:S(2)}, u32[]{:S(2)}) async-start(bf16[16,48,512]{2,1,0:T(8,128)(2,1)} %bitcast.9), calls=%async_computation | async-start | bytes 1572864 | tf_op jit(solution)/shard_map/all_to_all | solution.py:603
  12.1 0.8 dynamic-slice_bitcast_fusion.1
  14.6 22.6 %edge_start.1.partial = bf16[4,2560,512]{2,1,0:T(8,128)(2,1)} custom-call(f32[2,8,1280]{2,1,0:T(8,128)} %bitcast.51, bf16[4,2560,512]{2,1,0:T(8,128)(2,1)} %x_high.1, bf16[4,320,512]{2,1,0:T(8,128)(2,1)} %nodes.3, bf16[1536,512]{1,0:T(8,128)(2,1)} %first.5, f32[8,512]{1,0:T(8,128)} %stack.54.vec), custom_call_target="tpu_custom_call" | custom-call | flops 16106127360 | bytes 20971520 | tf_op jit(solution)/shard_map/edge_start/pallas_call | solution.py:774
  38.5 1.0 broadcast_select_fusion.1.arrived
  39.5 37.2 %edge_forward.1 = (bf16[4,2560,512]{2,1,0:T(8,128)(2,1)}, bf16[4,2560,512]{2,1,0:T(8,128)(2,1)}, bf16[4,2560,512]{2,1,0:T(8,128)(2,1)}, f32[4,2560,128]{2,1,0:T(...) custom-call(f32[2,8,1280]{2,1,0:T(8,128)} %bitcast.52, ...), custom_call_target="tpu_custom_call" | custom-call | flops 21474836480 | bytes 41943040 | tf_op jit(solution)/shard_map/edge_forward/pallas_call | solution.py:801
  76.7 6.9 %all-to-all-start.1 = ((bf16[32,48,512]{2,1,0:T(8,128)(2,1)}), bf16[32,48,512]{2,1,0:T(8,128)(2,1)S(1)}, u32[]{:S(2)}, u32[]{:S(2)}) async-start(bf16[32,48,512]{2,1,0:T(8,128)(2,1)} %bitcast.48), calls=%async_computation.1 | async-start | bytes 3145728 | tf_op jit(solution)/shard_map/all_to_all | solution.py:649
  83.6 49.0 %edge_backward.1 = (bf16[4,2560,512]{2,1,0:T(8,128)(2,1)}, f32[4,8,512]{2,1,0:T(8,128)}, bf16[4,320,512]{2,1,0:T(8,128)(2,1)}, bf16[768,512]{1,0:T(8,128)(2,1)},...) custom-call(f32[5,8,512]{2,1,0:T(8,128)} %bitcast.53, ...), custom_call_target="tpu_custom_call" | custom-call | flops 37580963840 | bytes 52428800 | tf_op jit(solution)/shard_map/edge_backward/pallas_call | solution.py:879
  132.7 7.0 %all-to-all-start.2 = ((bf16[16,48,512]{2,1,0:T(8,128)(2,1)}), bf16[16,48,512]{2,1,0:T(8,128)(2,1)S(1)}, u32[]{:S(2)}, u32[]{:S(2)}) async-start(bf16[16,48,512]{2,1,0:T(8,128)(2,1)} %get-tuple-element.62.after), calls=%async_computation.2 | async-start | bytes 1572864 | tf_op jit(solution)/shard_map/all_to_all | solution.py:603
  139.6 8.6 %edge_totals.1 = (f32[4,320,512]{2,1,0:T(8,128)}, bf16[2048,512]{1,0:T(8,128)(2,1)}) custom-call(bf16[4,320,512]{2,1,0:T(8,128)(2,1)} %get-tuple-element.54.local, bf16[4,320,512]{2,1,0:T(8,128)(2,1)} %get-tuple-element.55.received, bf16[768,512]{1,0:T(8,128)(2,1)} %get-tuple-element.56.remote, ...), custom_call_target="tpu_custom_call", output_to_operand_aliasing={{1}: (7, {})} | custom-call | tf_op jit(solution)/shard_map/edge_totals/pallas_call | solution.py:949
  148.3 2.4 %constant_dynamic-slice_fusion = bf16[1024,512]{1,0:T(8,128)(2,1)} fusion(bf16[2048,512]{1,0:T(8,128)(2,1)} %get-tuple-element.63, s32[]{:T(128)S(6)} %select_n.100), kind=kLoop, calls=%fused_computation.71 | loop fusion | bytes 2097156 | tf_op jit(solution)/shard_map/dynamic_slice | solution.py:684
  150.7 0.9 collective-permute-start.1
  151.7 0.8 dynamic-slice_bitcast_fusion
  152.8 1.6 reduce_sum.60
  154.5 1.5 add_convert_fusion
  156.0 1.1 pad_maximum_fusion.1.after
  157.1 1.2 collective-permute-done.2
  158.3 0.9 all-to-all-done.2
  159.3 5.0 %all-to-all-start.3 = ((bf16[8,144,512]{2,1,0:T(8,128)(2,1)}), bf16[8,144,512]{2,1,0:T(8,128)(2,1)S(1)}, u32[]{:S(2)}, u32[]{:S(2)}) async-start(bf16[8,144,512]{2,1,0:T(8,128)(2,1)} %pad_maximum_fusion.1.after), calls=%async_computation.3 | async-start | bytes 2359296 | tf_op jit(solution)/shard_map/all_to_all | solution.py:672
  164.3 15.5 %edge_gradient.1 = bf16[4,2560,512]{2,1,0:T(8,128)(2,1)} custom-call(bf16[4,2560,512]{2,1,0:T(8,128)(2,1)} %cot_high.1, bf16[4,2560,512]{2,1,0:T(8,128)(2,1)} %cot_high.1, bf16[4,2560,512]{2,1,0:T(8,128)(2,1)} %get-tuple-element.68.hid_low.hid_high, bf16[4,2560,512]{2,1,0:T(8,128)(2,1)} %get-tuple-element.68.hid_low.hid_high, bf16[1536,512]{1,0:T(8,128)(2,1)} %first.5, ...), custom_call_target="tpu_custom_call" | custom-call | flops 5368709120 | bytes 31457280 | tf_op jit(solution)/shard_map/edge_gradient/pallas_call | solution.py:978
  180.1 0.7 collective-permute-start.3
  180.9 7.8 %collective-permute-done.3 = bf16[192,512]{1,0:T(8,128)(2,1)S(1)} collective-permute-done((bf16[192,512]{1,0:T(8,128)(2,1)S(1)}, bf16[192,512]{1,0:T(8,128)(2,1)S(1)}, u32[]{:S(2)}, u32[]{:S(2)}) %collective-permute-start.3) | collective-permute-done | bytes 196640 | tf_op jit(solution)/shard_map/ppermute | solution.py:591
  188.8 1.4 broadcast_in_dim.88
  190.2 8.0 %all-to-all-start.4 = ((bf16[8,224,512]{2,1,0:T(8,128)(2,1)}), bf16[8,224,512]{2,1,0:T(8,128)(2,1)S(1)}, u32[]{:S(2)}, u32[]{:S(2)}) async-start(bf16[8,224,512]{2,1,0:T(8,128)(2,1)} %broadcast_in_dim.88), calls=%async_computation.4 | async-start | bytes 3670016 | tf_op jit(solution)/shard_map/all_to_all | solution.py:672
  198.2 1.2 fusion.1
  199.9 2.1 add.133
  202.0 15.0 %edge_outputs.1 = bf16[4,2560,512]{2,1,0:T(8,128)(2,1)} custom-call(f32[2,8,1280]{2,1,0:T(8,128)} %bitcast.54, bf16[4,2560,512]{2,1,0:T(8,128)(2,1)} %x_high.1, bf16[4,2560,512]{2,1,0:T(8,128)(2,1)} %x_high.1, bf16[4,2560,512]{2,1,0:T(8,128)(2,1)} %get-tuple-element.51.nrm.nrm_low.nrm_high, bf16[4,2560,512]{2,1,0:T(8,128)(2,1)} %get-tuple-element.51.nrm.nrm_low.nrm_high, ...), custom_call_target="tpu_custom_call" | custom-call | bytes 31457280 | tf_op jit(solution)/shard_map/edge_outputs/pallas_call | solution.py:1002
  217.1 4.4 %all-to-all-done.4 = bf16[8,224,512]{2,1,0:T(8,128)(2,1)S(1)} async-done(((bf16[8,224,512]{2,1,0:T(8,128)(2,1)}), bf16[8,224,512]{2,1,0:T(8,128)(2,1)S(1)}, u32[]{:S(2)}, u32[]{:S(2)}) %all-to-all-start.4) | async-done | bytes 1835040 | tf_op jit(solution)/shard_map/all_to_all | solution.py:672
  222.0 7.9 %all_to_all.30.totals = bf16[2,1808,512]{2,1,0:T(8,128)(2,1)S(1)} all-to-all(bf16[2,1808,512]{2,1,0:T(8,128)(2,1)S(1)} %broadcast_in_dim.89), channel_id=1, replica_groups=mesh['dp'=2,'graph'=16] {'dp'}, dimensions={0} | all-to-all | bytes 7405568 | tf_op jit(solution)/shard_map/all_to_all | solution.py:676
  230.0 0.7 fusion.22
  230.7 1.1 copy-done
  231.8 4.2 %unpack.1 = (f32[1536,512]{1,0:T(8,128)}, f32[512,512]{1,0:T(8,128)}, f32[1024,512]{1,0:T(8,128)}, f32[512,512]{1,0:T(8,128)}) custom-call(bf16[2,1808,512]{2,1,0:T(8,128)(2,1)} %copy-done), custom_call_target="tpu_custom_call" | custom-call | tf_op jit(solution)/shard_map/unpack/pallas_call | solution.py:1033
  (85 shorter events, 6.2 us)
Async XLA Ops:
  2.0 11.1 %copy-start.7 = (s32[2560]{0:T(1024)S(1)}, s32[2560]{0:T(1024)}, u32[]{:S(2)}) copy-start(s32[2560]{0:T(1024)} %param.38) | copy-start | bytes 30724
  2.0 11.1 %copy-start.8 = (s32[2560]{0:T(1024)S(1)}, s32[2560]{0:T(1024)}, u32[]{:S(2)}) copy-start(s32[2560]{0:T(1024)} %param.37) | copy-start | bytes 30724
  2.0 11.9 %copy-start.9 = (f32[512]{0:T(512)S(1)}, f32[512]{0:T(512)}, u32[]{:S(2)}) copy-start(f32[512]{0:T(512)} %param.23) | copy-start | bytes 6148
  2.0 11.9 %copy-start.10 = (f32[512]{0:T(512)S(1)}, f32[512]{0:T(512)}, u32[]{:S(2)}) copy-start(f32[512]{0:T(512)} %param.25) | copy-start | bytes 6148
  2.1 11.9 %copy-start.11 = (f32[512]{0:T(512)S(1)}, f32[512]{0:T(512)}, u32[]{:S(2)}) copy-start(f32[512]{0:T(512)} %param.26) | copy-start | bytes 6148
  2.1 11.9 %copy-start.12 = (f32[512]{0:T(512)S(1)}, f32[512]{0:T(512)}, u32[]{:S(2)}) copy-start(f32[512]{0:T(512)} %param.27) | copy-start | bytes 6148
  5.5 32.9 %all-to-all-start = ((bf16[16,48,512]{2,1,0:T(8,128)(2,1)}), bf16[16,48,512]{2,1,0:T(8,128)(2,1)S(1)}, u32[]{:S(2)}, u32[]{:S(2)}) async-start(bf16[16,48,512]{2,1,0:T(8,128)(2,1)} %bitcast.9), calls=%async_computation | async-start | bytes 1572864 | tf_op jit(solution)/shard_map/all_to_all | solution.py:603
  12.9 25.6 %collective-permute-start = (bf16[48,512]{1,0:T(8,128)(2,1)S(1)}, bf16[48,512]{1,0:T(8,128)(2,1)S(1)}, u32[]{:S(2)}, u32[]{:S(2)}) collective-permute-start(bf16[48,512]{1,0:T(8,128)(2,1)S(1)} %dynamic-slice_bitcast_fusion.1), channel_id=1, source_target_pairs={{0,8},{1,9},{2,10},{3,11},{4,12},{5,13},{6,14},{7,15},{8,0},{9,1},... | collective-permute-start | bytes 147464 | tf_op jit(solution)/shard_map/ppermute | solution.py:591
  14.6 22.6 %copy-start.17 = (s32[320]{0:T(512)S(1)}, s32[320]{0:T(512)}, u32[]{:S(2)}) copy-start(s32[320]{0:T(512)} %param.39) | copy-start | bytes 3844
  14.6 23.2 %copy-start.13 = (f32[512]{0:T(512)S(1)}, f32[512]{0:T(512)}, u32[]{:S(2)}) copy-start(f32[512]{0:T(512)} %param.29) | copy-start | bytes 6148
  14.6 23.2 %copy-start.14 = (f32[512]{0:T(512)S(1)}, f32[512]{0:T(512)}, u32[]{:S(2)}) copy-start(f32[512]{0:T(512)} %param.31) | copy-start | bytes 6148
  14.6 23.2 %copy-start.15 = (f32[512]{0:T(512)S(1)}, f32[512]{0:T(512)}, u32[]{:S(2)}) copy-start(f32[512]{0:T(512)} %param.32) | copy-start | bytes 6148
  14.6 23.2 %copy-start.16 = (f32[512]{0:T(512)S(1)}, f32[512]{0:T(512)}, u32[]{:S(2)}) copy-start(f32[512]{0:T(512)} %param.33) | copy-start | bytes 6148
  76.7 55.9 %all-to-all-start.1 = ((bf16[32,48,512]{2,1,0:T(8,128)(2,1)}), bf16[32,48,512]{2,1,0:T(8,128)(2,1)S(1)}, u32[]{:S(2)}, u32[]{:S(2)}) async-start(bf16[32,48,512]{2,1,0:T(8,128)(2,1)} %bitcast.48), calls=%async_computation.1 | async-start | bytes 3145728 | tf_op jit(solution)/shard_map/all_to_all | solution.py:649
  132.6 7.0 %copy-start.2 = (bf16[32,48,512]{2,1,0:T(8,128)(2,1)}, bf16[32,48,512]{2,1,0:T(8,128)(2,1)S(1)}, u32[]{:S(2)}) copy-start(bf16[32,48,512]{2,1,0:T(8,128)(2,1)S(1)} %all-to-all-done.1) | copy-start | bytes 4718596
  132.7 26.6 %all-to-all-start.2 = ((bf16[16,48,512]{2,1,0:T(8,128)(2,1)}), bf16[16,48,512]{2,1,0:T(8,128)(2,1)S(1)}, u32[]{:S(2)}, u32[]{:S(2)}) async-start(bf16[16,48,512]{2,1,0:T(8,128)(2,1)} %get-tuple-element.62.after), calls=%async_computation.2 | async-start | bytes 1572864 | tf_op jit(solution)/shard_map/all_to_all | solution.py:603
  139.6 12.0 %copy-start.5 = (f32[4,8,512]{2,1,0:T(8,128)S(1)}, f32[4,8,512]{2,1,0:T(8,128)}, u32[]{:S(2)}) copy-start(f32[4,8,512]{2,1,0:T(8,128)} %get-tuple-element.65) | copy-start | bytes 196612
  139.6 12.0 %copy-start.6 = (f32[4,8,512]{2,1,0:T(8,128)S(1)}, f32[4,8,512]{2,1,0:T(8,128)}, u32[]{:S(2)}) copy-start(f32[4,8,512]{2,1,0:T(8,128)} %get-tuple-element.64) | copy-start | bytes 196612
  148.3 6.2 %copy-start.1 = (bf16[2048,512]{1,0:T(8,128)(2,1)S(1)}, bf16[2048,512]{1,0:T(8,128)(2,1)}, u32[]{:S(2)}) copy-start(bf16[2048,512]{1,0:T(8,128)(2,1)} %get-tuple-element.63) | copy-start | bytes 6291460
  150.7 3.7 %collective-permute-start.1 = (bf16[1024,512]{1,0:T(8,128)(2,1)}, bf16[1024,512]{1,0:T(8,128)(2,1)}, u32[]{:S(2)}, u32[]{:S(2)}) collective-permute-start(bf16[1024,512]{1,0:T(8,128)(2,1)} %constant_dynamic-slice_fusion), channel_id=1, source_target_pairs={{0,16},{16,0},{1,17},{17,1},{2,18},{18,2},{3,19},{19,3},{4,20},{20... | collective-permute-start | bytes 3145736 | tf_op jit(solution)/shard_map/ppermute | solution.py:685
  152.5 5.8 %collective-permute-start.2 = (bf16[48,512]{1,0:T(8,128)(2,1)S(1)}, bf16[48,512]{1,0:T(8,128)(2,1)S(1)}, u32[]{:S(2)}, u32[]{:S(2)}) collective-permute-start(bf16[48,512]{1,0:T(8,128)(2,1)S(1)} %dynamic-slice_bitcast_fusion), channel_id=1, source_target_pairs={{0,8},{1,9},{2,10},{3,11},{4,12},{5,13},{6,14},{7,15},{8,0},{9,1},... | collective-permute-start | bytes 147464 | tf_op jit(solution)/shard_map/ppermute | solution.py:591
  159.3 20.5 %all-to-all-start.3 = ((bf16[8,144,512]{2,1,0:T(8,128)(2,1)}), bf16[8,144,512]{2,1,0:T(8,128)(2,1)S(1)}, u32[]{:S(2)}, u32[]{:S(2)}) async-start(bf16[8,144,512]{2,1,0:T(8,128)(2,1)} %pad_maximum_fusion.1.after), calls=%async_computation.3 | async-start | bytes 2359296 | tf_op jit(solution)/shard_map/all_to_all | solution.py:672
  180.1 8.6 %collective-permute-start.3 = (bf16[192,512]{1,0:T(8,128)(2,1)S(1)}, bf16[192,512]{1,0:T(8,128)(2,1)S(1)}, u32[]{:S(2)}, u32[]{:S(2)}) collective-permute-start(bf16[192,512]{1,0:T(8,128)(2,1)S(1)} %pad_maximum_fusion.4), channel_id=1, source_target_pairs={{0,8},{1,9},{2,10},{3,11},{4,12},{5,13},{6,14},{7,15},{8,0},{9,1},... | collective-permute-start | bytes 589832 | tf_op jit(solution)/shard_map/ppermute | solution.py:591
  188.8 1.4 copy-start.4
  190.2 31.2 %all-to-all-start.4 = ((bf16[8,224,512]{2,1,0:T(8,128)(2,1)}), bf16[8,224,512]{2,1,0:T(8,128)(2,1)S(1)}, u32[]{:S(2)}, u32[]{:S(2)}) async-start(bf16[8,224,512]{2,1,0:T(8,128)(2,1)} %broadcast_in_dim.88), calls=%async_computation.4 | async-start | bytes 3670016 | tf_op jit(solution)/shard_map/all_to_all | solution.py:672
  198.2 1.7 copy-start.3
  230.0 1.8 copy-start

commit v2 on v1

--- a/solution.py
+++ b/solution.py
@@ -96,7 +96,7 @@
 
 
 def edge_forward(
-    idx, count, partial, arrived, send, second, vec, node_vec,
+    idx, mask, partial, arrived, send, second, vec,
     nodes_hbm, cot_hbm, node_first_hbm, node_second_hbm,
     act, bend, nrm, inv, vec_grad, nodes_out_hbm, base_hbm, gathered_grad_hbm, weight_grad_hbm,
     inputs, picks, table, live, degree, sums, node_inputs, node_actives, pre_grads, hidden_grads,
@@ -194,7 +194,7 @@
         for copy in incoming:
             copy.wait()
         lines = lax.broadcasted_iota(jnp.int32, (here, 1), 0)
-        alive = jnp.where(lines < count[0], 1.0, 0.0)
+        alive = jnp.where(lines.astype(F32) < jnp.sum(mask[...].astype(F32)), 1.0, 0.0)
         shifts = lanes(degree[...], width) * vec[3:4]
         vectors = [jnp.zeros((8, width), F32) for _ in range(4)]
         hidden, pre, back = {}, {}, {}
@@ -208,20 +208,20 @@
         def second_layer(s):
             for row in range(0, here, BLOCK):
                 at = slice(s * here + row, s * here + row + BLOCK)
-                value = hidden[s][row : row + BLOCK] + node_vec[0:1]
+                value = hidden[s][row : row + BLOCK] + vec[4:5]
                 node_actives[at] = (value * logistic(value)).astype(BF16)
             pre[s] = dot(node_actives[s * here : (s + 1) * here], node_second[...])
 
         def norm(s):
             for row in range(0, here, BLOCK):
                 inside = slice(row, row + BLOCK)
-                normed, inverse = normalize(pre[s][inside] + node_vec[1:2])
-                update = alive[inside] * (normed * node_vec[2:3] + node_vec[3:4])
+                normed, inverse = normalize(pre[s][inside] + vec[5:6])
+                update = alive[inside] * (normed * vec[6:7] + vec[7:8])
                 nodes_out[s, inside] = (nodes[s, inside].astype(F32) + update).astype(BF16)
                 out_grad = alive[inside] * cot[s, inside].astype(F32)
                 vectors[2] += fold(out_grad * normed)
                 vectors[3] += fold(out_grad)
-                pre_grad = norm_back(out_grad * node_vec[2:3], normed, inverse)
+                pre_grad = norm_back(out_grad * vec[6:7], normed, inverse)
                 vectors[1] += fold(pre_grad)
                 pre_grads[s * here + row : s * here + row + BLOCK] = pre_grad.astype(BF16)
             pltpu.make_async_copy(nodes_out.at[s], nodes_out_hbm.at[s], leave.at[s]).start()
@@ -230,7 +230,7 @@
         def first_back(s):
             for row in range(0, here, BLOCK):
                 at = slice(s * here + row, s * here + row + BLOCK)
-                value = hidden[s][row : row + BLOCK] + node_vec[0:1]
+                value = hidden[s][row : row + BLOCK] + vec[4:5]
                 sigma = logistic(value)
                 hidden_grad = back[s][row : row + BLOCK] * (sigma + value * sigma * (1.0 - sigma))
                 vectors[0] += fold(hidden_grad)
@@ -534,8 +534,8 @@
 
 
 def unpack(totals, *refs):
-    outs, (taken, given, arrive, leave) = refs[:-4], refs[-4:]
-    rows = taken.shape[1]
+    outs, (given, leave) = refs[:-2], refs[-2:]
+    rows = given.shape[1]
     width = totals.shape[2]
     edge_half, node_half = 2 * width, (totals.shape[1] - 2 * width) // rows * rows
     places = []
@@ -547,20 +547,12 @@
                     places.append((core, start + row, pair[0], goal))
                 else:
                     places.append((core, start + row, pair[1], goal - pair[0].shape[0]))
-    incoming = [
-        pltpu.make_async_copy(totals.at[core, pl.ds(row, rows)], taken.at[n], arrive.at[n])
-        for n, (core, row, _, _) in enumerate(places)
-    ]
-    leaving = [
-        pltpu.make_async_copy(given.at[n], goal.at[pl.ds(row, rows)], leave.at[n])
-        for n, (_, _, goal, row) in enumerate(places)
-    ]
-    for copy in incoming:
+    leaving = []
+    for n, (core, row, target, goal) in enumerate(places):
+        given[n] = totals[core, row : row + rows].astype(F32)
+        copy = pltpu.make_async_copy(given.at[n], target.at[pl.ds(goal, rows)], leave.at[n])
         copy.start()
-    for n in range(len(places)):
-        incoming[n].wait()
-        given[n] = taken[n].astype(F32)
-        leaving[n].start()
+        leaving.append(copy)
     for copy in leaving:
         copy.wait()
 
@@ -732,12 +724,9 @@
         ]
     )
     idx = jnp.pad(idx, ((0, 5), (0, 0)))
-    zero = jnp.zeros((width,), F32)
-    edge_vec = jnp.stack(
-        [edge_first_bias, edge_second_bias, edge_gain, edge_shift, zero, zero, zero, zero]
-    )
-    node_vec = jnp.stack(
-        [node_first_bias, node_second_bias, node_gain, node_shift, zero, zero, zero, zero]
+    vec = jnp.stack(
+        [edge_first_bias, edge_second_bias, edge_gain, edge_shift]
+        + [node_first_bias, node_second_bias, node_gain, node_shift]
     )
     unit = 2 * samples * edges * width * width
 
@@ -792,9 +781,8 @@
             flops=3 * unit, bytes_accessed=4 * samples * edges * width, transcendentals=0
         ),
         name="edge_start",
-    )(tiled(wide), edge_latents, node_latents, edge_first, edge_vec)
-
-    count = jnp.sum(node_mask).reshape(1)
+    )(tiled(wide), edge_latents, node_latents, edge_first, vec)
+
     remote = -(-far // 128) * 128
     (
         act, bend, nrm, inv, node_sums, nodes_out, base, gathered_grad, node_weights
@@ -803,12 +791,11 @@
         grid=(edges // wide, samples),
         in_specs=[
             idx_block(wide),
-            pl.BlockSpec(memory_space=pltpu.SMEM),
+            whole((1, here)),
             edge_block(wide),
             whole((near, samples * slots, width)),
             third(1),
             whole((width, width)),
-            whole((8, width)),
             whole((8, width)),
         ]
         + [unread()] * 4,
@@ -856,7 +843,7 @@
         ),
         name="edge_forward",
     )(
-        tiled(wide), count, partial, arrived, edge_first, edge_second, edge_vec, node_vec,
+        tiled(wide), node_mask[None], partial, arrived, edge_first, edge_second, vec,
         node_latents, node_cot, node_first, node_second,
     )
     node_parts = scatter_all(node_weights)
@@ -939,7 +926,7 @@
         name="edge_backward",
     )(
         tiled(short), edge_latents, edge_latents, edge_cot, act, act, bend, nrm, inv,
-        gathered_grad, edge_second, edge_vec,
+        gathered_grad, edge_second, vec,
         edge_latents, act, edge_first,
     )
     node_parts, edge_weights, outbound = lax.optimization_barrier(
@@ -1018,7 +1005,7 @@
         ),
         name="edge_outputs",
     )(
-        tiled(wide), edge_latents, edge_latents, nrm, nrm, edge_vec, joined,
+        tiled(wide), edge_latents, edge_latents, nrm, nrm, vec, joined,
     )
     gathered_rows, edges_out = lax.optimization_barrier((gathered_rows, edges_out))
     nodes_rows = gathered_rows[:, piece:]
@@ -1032,15 +1019,13 @@
     parts = 7 * width // chunk
     weights = pl.pallas_call(
         unpack,
-        in_specs=[unread()],
+        in_specs=[pl.BlockSpec(memory_space=pltpu.VMEM)],
         out_specs=[unread()] * 4,
         out_shape=[
             jax.ShapeDtypeStruct((rows * width, width), F32) for rows in (3, 1, 2, 1)
         ],
         scratch_shapes=[
-            pltpu.VMEM((parts, chunk, width), BF16),
             pltpu.VMEM((parts, chunk, width), F32),
-            pltpu.SemaphoreType.DMA((parts,)),
             pltpu.SemaphoreType.DMA((parts,)),
         ],
         compiler_params=pltpu.CompilerParams(vmem_limit_bytes=VMEM),

time: 237 us -> 236 us (level)
  no operation moved by 1% of the time
where the time goes in v2:
time: 236 us; the launch traced here: 235 us
  Pallas kernels  152 us (64%)
  starting transfers between devices  35.3 us (15%)
  waiting for transfers between devices  14.3 us (6%)
  local copies, waits for them, and re-layouts  10.3 us (4%)
  other arithmetic  9.12 us (4%)
  blocking collectives  7.93 us (3%)
  matrix products  4.69 us (2%)
    pallas_call x1, Pallas kernels, shards(): pl.pallas_call(edge_backward, grid=(edges // short * pairs,), in_specs=[p...  49 us
    pallas_call x1, Pallas kernels, shards(): pl.pallas_call(edge_forward, grid=(edges // wide, samples), in_specs=[idx...  36.3 us
    pallas_call x1, Pallas kernels, shards(): pl.pallas_call(edge_start, grid=(edges // wide, samples), in_specs=[idx_b...  22.5 us
    pallas_call x1, Pallas kernels, shards(): pl.pallas_call(edge_gradient, grid=(edges // wide, samples), in_specs=[*t...  15.5 us
    pallas_call x1, Pallas kernels, shards(): pl.pallas_call(edge_outputs, grid=(edges // wide, samples), in_specs=[idx...  15.1 us
    all_to_all x2, starting transfers between devices, exchange(): swapped = lax.all_to_all(chunks, 'graph', 0, 0)  13.2 us
    all_to_all x2, starting transfers between devices, exchange_in_side(): lax.all_to_all(pieces, 'graph', 0, 0, axis_index_groups=side_groups())  13 us
    ppermute x3, waiting for transfers between devices, shift(): lax.ppermute(block, 'graph', [(i, (i + distance) % size) for i in range(s...  9.06 us
  transfers between devices with their start and end apart: 9, of which 4 were waited for; matrix products, arithmetic and copies ran while one was open for 6% of the time, Pallas kernels for 47%

profile of v2, /device:TPU:19, one launch (start us, length us, event | category | flops | bytes accessed | tf_op | source)
XLA Modules:
  0.0 235.3 jit_solution(17763642345629921390)
XLA Ops:
  2.1 3.5 %fusion.6 = bf16[768,512]{1,0:T(8,128)(2,1)} fusion(bf16[1280,512]{1,0:T(8,128)(2,1)} %bitcast.48, s32[768]{0:T(1024)S(1)} %add.126), kind=kOutput, calls=%fused_computation.10 | convolution fusion | flops 1008009216 | bytes 2100224 | tf_op jit(solution)/shard_map/dot_general | solution.py:19
  5.6 6.5 %all-to-all-start = ((bf16[16,48,512]{2,1,0:T(8,128)(2,1)}), bf16[16,48,512]{2,1,0:T(8,128)(2,1)S(1)}, u32[]{:S(2)}, u32[]{:S(2)}) async-start(bf16[16,48,512]{2,1,0:T(8,128)(2,1)} %bitcast.12), calls=%async_computation | async-start | bytes 1572864 | tf_op jit(solution)/shard_map/all_to_all | solution.py:595
  12.1 0.8 dynamic-slice_bitcast_fusion.1
  14.7 22.5 %edge_start.1.partial = bf16[4,2560,512]{2,1,0:T(8,128)(2,1)} custom-call(f32[2,8,1280]{2,1,0:T(8,128)} %bitcast.50, bf16[4,2560,512]{2,1,0:T(8,128)(2,1)} %x_high.1, bf16[4,320,512]{2,1,0:T(8,128)(2,1)} %nodes.3, bf16[1536,512]{1,0:T(8,128)(2,1)} %first.5, f32[8,512]{1,0:T(8,128)} %stack.55.vec), custom_call_target="tpu_custom_call" | custom-call | flops 16106127360 | bytes 20971520 | tf_op jit(solution)/shard_map/edge_start/pallas_call | solution.py:763
  37.8 1.0 broadcast_select_fusion.1.arrived
  38.8 36.3 %edge_forward.1 = (bf16[4,2560,512]{2,1,0:T(8,128)(2,1)}, bf16[4,2560,512]{2,1,0:T(8,128)(2,1)}, bf16[4,2560,512]{2,1,0:T(8,128)(2,1)}, f32[4,2560,128]{2,1,0:T(...) custom-call(f32[2,8,1280]{2,1,0:T(8,128)} %bitcast.51, ...), custom_call_target="tpu_custom_call" | custom-call | flops 21474836480 | bytes 41943040 | tf_op jit(solution)/shard_map/edge_forward/pallas_call | solution.py:789
  75.1 6.9 %all-to-all-start.1 = ((bf16[32,48,512]{2,1,0:T(8,128)(2,1)}), bf16[32,48,512]{2,1,0:T(8,128)(2,1)S(1)}, u32[]{:S(2)}, u32[]{:S(2)}) async-start(bf16[32,48,512]{2,1,0:T(8,128)(2,1)} %bitcast.47), calls=%async_computation.1 | async-start | bytes 3145728 | tf_op jit(solution)/shard_map/all_to_all | solution.py:641
  82.0 49.0 %edge_backward.1 = (bf16[4,2560,512]{2,1,0:T(8,128)(2,1)}, f32[4,8,512]{2,1,0:T(8,128)}, bf16[4,320,512]{2,1,0:T(8,128)(2,1)}, bf16[768,512]{1,0:T(8,128)(2,1)},...) custom-call(f32[5,8,512]{2,1,0:T(8,128)} %bitcast.52, ...), custom_call_target="tpu_custom_call" | custom-call | flops 37580963840 | bytes 52428800 | tf_op jit(solution)/shard_map/edge_backward/pallas_call | solution.py:866
  131.0 6.7 %all-to-all-start.2 = ((bf16[16,48,512]{2,1,0:T(8,128)(2,1)}), bf16[16,48,512]{2,1,0:T(8,128)(2,1)S(1)}, u32[]{:S(2)}, u32[]{:S(2)}) async-start(bf16[16,48,512]{2,1,0:T(8,128)(2,1)} %get-tuple-element.62.after), calls=%async_computation.2 | async-start | bytes 1572864 | tf_op jit(solution)/shard_map/all_to_all | solution.py:595
  137.8 8.6 %edge_totals.1 = (f32[4,320,512]{2,1,0:T(8,128)}, bf16[2048,512]{1,0:T(8,128)(2,1)}) custom-call(bf16[4,320,512]{2,1,0:T(8,128)(2,1)} %get-tuple-element.54.local, bf16[4,320,512]{2,1,0:T(8,128)(2,1)} %get-tuple-element.55.received, bf16[768,512]{1,0:T(8,128)(2,1)} %get-tuple-element.56.remote, ...), custom_call_target="tpu_custom_call", output_to_operand_aliasing={{1}: (7, {})} | custom-call | tf_op jit(solution)/shard_map/edge_totals/pallas_call | solution.py:936
  146.4 2.4 %constant_dynamic-slice_fusion = bf16[1024,512]{1,0:T(8,128)(2,1)} fusion(bf16[2048,512]{1,0:T(8,128)(2,1)} %get-tuple-element.63, s32[]{:T(128)S(6)} %select_n.100), kind=kLoop, calls=%fused_computation.71 | loop fusion | bytes 2097156 | tf_op jit(solution)/shard_map/dynamic_slice | solution.py:676
  148.8 0.9 collective-permute-start.1
  149.8 0.8 dynamic-slice_bitcast_fusion
  150.9 1.6 reduce_sum.50
  152.6 1.5 add_convert_fusion
  154.1 1.1 pad_maximum_fusion.1.after
  155.2 1.2 collective-permute-done.2
  156.4 0.9 all-to-all-done.2
  157.5 5.0 %all-to-all-start.3 = ((bf16[8,144,512]{2,1,0:T(8,128)(2,1)}), bf16[8,144,512]{2,1,0:T(8,128)(2,1)S(1)}, u32[]{:S(2)}, u32[]{:S(2)}) async-start(bf16[8,144,512]{2,1,0:T(8,128)(2,1)} %pad_maximum_fusion.1.after), calls=%async_computation.3 | async-start | bytes 2359296 | tf_op jit(solution)/shard_map/all_to_all | solution.py:664
  162.5 15.5 %edge_gradient.1 = bf16[4,2560,512]{2,1,0:T(8,128)(2,1)} custom-call(bf16[4,2560,512]{2,1,0:T(8,128)(2,1)} %cot_high.1, bf16[4,2560,512]{2,1,0:T(8,128)(2,1)} %cot_high.1, bf16[4,2560,512]{2,1,0:T(8,128)(2,1)} %get-tuple-element.68.hid_low.hid_high, bf16[4,2560,512]{2,1,0:T(8,128)(2,1)} %get-tuple-element.68.hid_low.hid_high, bf16[1536,512]{1,0:T(8,128)(2,1)} %first.5, ...), custom_call_target="tpu_custom_call" | custom-call | flops 5368709120 | bytes 31457280 | tf_op jit(solution)/shard_map/edge_gradient/pallas_call | solution.py:965
  178.2 0.7 collective-permute-start.3
  179.0 7.8 %collective-permute-done.3 = bf16[192,512]{1,0:T(8,128)(2,1)S(1)} collective-permute-done((bf16[192,512]{1,0:T(8,128)(2,1)S(1)}, bf16[192,512]{1,0:T(8,128)(2,1)S(1)}, u32[]{:S(2)}, u32[]{:S(2)}) %collective-permute-start.3) | collective-permute-done | bytes 196640 | tf_op jit(solution)/shard_map/ppermute | solution.py:583
  187.0 1.4 broadcast_in_dim.92
  188.3 8.0 %all-to-all-start.4 = ((bf16[8,224,512]{2,1,0:T(8,128)(2,1)}), bf16[8,224,512]{2,1,0:T(8,128)(2,1)S(1)}, u32[]{:S(2)}, u32[]{:S(2)}) async-start(bf16[8,224,512]{2,1,0:T(8,128)(2,1)} %broadcast_in_dim.92), calls=%async_computation.4 | async-start | bytes 3670016 | tf_op jit(solution)/shard_map/all_to_all | solution.py:664
  196.3 1.2 fusion.1
  198.0 2.1 add.133
  200.1 15.1 %edge_outputs.1 = bf16[4,2560,512]{2,1,0:T(8,128)(2,1)} custom-call(f32[2,8,1280]{2,1,0:T(8,128)} %bitcast.53, bf16[4,2560,512]{2,1,0:T(8,128)(2,1)} %x_high.1, bf16[4,2560,512]{2,1,0:T(8,128)(2,1)} %x_high.1, bf16[4,2560,512]{2,1,0:T(8,128)(2,1)} %get-tuple-element.51.nrm.nrm_low.nrm_high, bf16[4,2560,512]{2,1,0:T(8,128)(2,1)} %get-tuple-element.51.nrm.nrm_low.nrm_high, ...), custom_call_target="tpu_custom_call" | custom-call | bytes 31457280 | tf_op jit(solution)/shard_map/edge_outputs/pallas_call | solution.py:989
  215.2 4.4 %all-to-all-done.4 = bf16[8,224,512]{2,1,0:T(8,128)(2,1)S(1)} async-done(((bf16[8,224,512]{2,1,0:T(8,128)(2,1)}), bf16[8,224,512]{2,1,0:T(8,128)(2,1)S(1)}, u32[]{:S(2)}, u32[]{:S(2)}) %all-to-all-start.4) | async-done | bytes 1835040 | tf_op jit(solution)/shard_map/all_to_all | solution.py:664
  220.2 7.9 %all_to_all.30.totals = bf16[2,1808,512]{2,1,0:T(8,128)(2,1)S(1)} all-to-all(bf16[2,1808,512]{2,1,0:T(8,128)(2,1)S(1)} %broadcast_in_dim.93), channel_id=1, replica_groups=mesh['dp'=2,'graph'=16] {'dp'}, dimensions={0} | all-to-all | bytes 7405568 | tf_op jit(solution)/shard_map/all_to_all | solution.py:668
  228.1 0.7 fusion.22
  228.8 1.1 copy-done
  229.9 5.2 %unpack.1 = (f32[1536,512]{1,0:T(8,128)}, f32[512,512]{1,0:T(8,128)}, f32[1024,512]{1,0:T(8,128)}, f32[512,512]{1,0:T(8,128)}) custom-call(bf16[2,1808,512]{2,1,0:T(8,128)(2,1)} %copy-done), custom_call_target="tpu_custom_call" | custom-call | tf_op jit(solution)/shard_map/unpack/pallas_call | solution.py:1020
  (83 shorter events, 5.5 us)
Async XLA Ops:
  2.0 11.2 %copy-start.7 = (s32[2560]{0:T(1024)S(1)}, s32[2560]{0:T(1024)}, u32[]{:S(2)}) copy-start(s32[2560]{0:T(1024)} %param.38) | copy-start | bytes 30724
  2.0 11.2 %copy-start.8 = (s32[2560]{0:T(1024)S(1)}, s32[2560]{0:T(1024)}, u32[]{:S(2)}) copy-start(s32[2560]{0:T(1024)} %param.37) | copy-start | bytes 30724
  2.0 12.0 %copy-start.9 = (f32[512]{0:T(512)S(1)}, f32[512]{0:T(512)}, u32[]{:S(2)}) copy-start(f32[512]{0:T(512)} %param.23) | copy-start | bytes 6148
  2.0 11.9 %copy-start.10 = (f32[512]{0:T(512)S(1)}, f32[512]{0:T(512)}, u32[]{:S(2)}) copy-start(f32[512]{0:T(512)} %param.25) | copy-start | bytes 6148
  2.1 11.9 %copy-start.11 = (f32[512]{0:T(512)S(1)}, f32[512]{0:T(512)}, u32[]{:S(2)}) copy-start(f32[512]{0:T(512)} %param.26) | copy-start | bytes 6148
  2.1 11.9 %copy-start.12 = (f32[512]{0:T(512)S(1)}, f32[512]{0:T(512)}, u32[]{:S(2)}) copy-start(f32[512]{0:T(512)} %param.27) | copy-start | bytes 6148
  2.1 11.9 %copy-start.13 = (f32[512]{0:T(512)S(1)}, f32[512]{0:T(512)}, u32[]{:S(2)}) copy-start(f32[512]{0:T(512)} %param.29) | copy-start | bytes 6148
  2.1 11.9 %copy-start.14 = (f32[512]{0:T(512)S(1)}, f32[512]{0:T(512)}, u32[]{:S(2)}) copy-start(f32[512]{0:T(512)} %param.31) | copy-start | bytes 6148
  2.1 11.9 %copy-start.15 = (f32[512]{0:T(512)S(1)}, f32[512]{0:T(512)}, u32[]{:S(2)}) copy-start(f32[512]{0:T(512)} %param.32) | copy-start | bytes 6148
  2.1 11.9 %copy-start.16 = (f32[512]{0:T(512)S(1)}, f32[512]{0:T(512)}, u32[]{:S(2)}) copy-start(f32[512]{0:T(512)} %param.33) | copy-start | bytes 6148
  5.6 32.2 %all-to-all-start = ((bf16[16,48,512]{2,1,0:T(8,128)(2,1)}), bf16[16,48,512]{2,1,0:T(8,128)(2,1)S(1)}, u32[]{:S(2)}, u32[]{:S(2)}) async-start(bf16[16,48,512]{2,1,0:T(8,128)(2,1)} %bitcast.12), calls=%async_computation | async-start | bytes 1572864 | tf_op jit(solution)/shard_map/all_to_all | solution.py:595
  12.9 24.9 %collective-permute-start = (bf16[48,512]{1,0:T(8,128)(2,1)S(1)}, bf16[48,512]{1,0:T(8,128)(2,1)S(1)}, u32[]{:S(2)}, u32[]{:S(2)}) collective-permute-start(bf16[48,512]{1,0:T(8,128)(2,1)S(1)} %dynamic-slice_bitcast_fusion.1), channel_id=1, source_target_pairs={{0,8},{1,9},{2,10},{3,11},{4,12},{5,13},{6,14},{7,15},{8,0},{9,1},... | collective-permute-start | bytes 147464 | tf_op jit(solution)/shard_map/ppermute | solution.py:583
  14.7 22.5 %copy-start.17 = (s32[320]{0:T(512)S(1)}, s32[320]{0:T(512)}, u32[]{:S(2)}) copy-start(s32[320]{0:T(512)} %param.39) | copy-start | bytes 3844
  75.1 55.9 %all-to-all-start.1 = ((bf16[32,48,512]{2,1,0:T(8,128)(2,1)}), bf16[32,48,512]{2,1,0:T(8,128)(2,1)S(1)}, u32[]{:S(2)}, u32[]{:S(2)}) async-start(bf16[32,48,512]{2,1,0:T(8,128)(2,1)} %bitcast.47), calls=%async_computation.1 | async-start | bytes 3145728 | tf_op jit(solution)/shard_map/all_to_all | solution.py:641
  131.0 6.7 %copy-start.2 = (bf16[32,48,512]{2,1,0:T(8,128)(2,1)}, bf16[32,48,512]{2,1,0:T(8,128)(2,1)S(1)}, u32[]{:S(2)}) copy-start(bf16[32,48,512]{2,1,0:T(8,128)(2,1)S(1)} %all-to-all-done.1) | copy-start | bytes 4718596
  131.0 26.3 %all-to-all-start.2 = ((bf16[16,48,512]{2,1,0:T(8,128)(2,1)}), bf16[16,48,512]{2,1,0:T(8,128)(2,1)S(1)}, u32[]{:S(2)}, u32[]{:S(2)}) async-start(bf16[16,48,512]{2,1,0:T(8,128)(2,1)} %get-tuple-element.62.after), calls=%async_computation.2 | async-start | bytes 1572864 | tf_op jit(solution)/shard_map/all_to_all | solution.py:595
  137.7 12.0 %copy-start.5 = (f32[4,8,512]{2,1,0:T(8,128)S(1)}, f32[4,8,512]{2,1,0:T(8,128)}, u32[]{:S(2)}) copy-start(f32[4,8,512]{2,1,0:T(8,128)} %get-tuple-element.65) | copy-start | bytes 196612
  137.7 12.0 %copy-start.6 = (f32[4,8,512]{2,1,0:T(8,128)S(1)}, f32[4,8,512]{2,1,0:T(8,128)}, u32[]{:S(2)}) copy-start(f32[4,8,512]{2,1,0:T(8,128)} %get-tuple-element.64) | copy-start | bytes 196612
  146.4 6.2 %copy-start.1 = (bf16[2048,512]{1,0:T(8,128)(2,1)S(1)}, bf16[2048,512]{1,0:T(8,128)(2,1)}, u32[]{:S(2)}) copy-start(bf16[2048,512]{1,0:T(8,128)(2,1)} %get-tuple-element.63) | copy-start | bytes 6291460
  148.8 3.7 %collective-permute-start.1 = (bf16[1024,512]{1,0:T(8,128)(2,1)}, bf16[1024,512]{1,0:T(8,128)(2,1)}, u32[]{:S(2)}, u32[]{:S(2)}) collective-permute-start(bf16[1024,512]{1,0:T(8,128)(2,1)} %constant_dynamic-slice_fusion), channel_id=1, source_target_pairs={{0,16},{16,0},{1,17},{17,1},{2,18},{18,2},{3,19},{19,3},{4,20},{20... | collective-permute-start | bytes 3145736 | tf_op jit(solution)/shard_map/ppermute | solution.py:677
  150.7 5.8 %collective-permute-start.2 = (bf16[48,512]{1,0:T(8,128)(2,1)S(1)}, bf16[48,512]{1,0:T(8,128)(2,1)S(1)}, u32[]{:S(2)}, u32[]{:S(2)}) collective-permute-start(bf16[48,512]{1,0:T(8,128)(2,1)S(1)} %dynamic-slice_bitcast_fusion), channel_id=1, source_target_pairs={{0,8},{1,9},{2,10},{3,11},{4,12},{5,13},{6,14},{7,15},{8,0},{9,1},... | collective-permute-start | bytes 147464 | tf_op jit(solution)/shard_map/ppermute | solution.py:583
  157.5 20.5 %all-to-all-start.3 = ((bf16[8,144,512]{2,1,0:T(8,128)(2,1)}), bf16[8,144,512]{2,1,0:T(8,128)(2,1)S(1)}, u32[]{:S(2)}, u32[]{:S(2)}) async-start(bf16[8,144,512]{2,1,0:T(8,128)(2,1)} %pad_maximum_fusion.1.after), calls=%async_computation.3 | async-start | bytes 2359296 | tf_op jit(solution)/shard_map/all_to_all | solution.py:664
  178.2 8.6 %collective-permute-start.3 = (bf16[192,512]{1,0:T(8,128)(2,1)S(1)}, bf16[192,512]{1,0:T(8,128)(2,1)S(1)}, u32[]{:S(2)}, u32[]{:S(2)}) collective-permute-start(bf16[192,512]{1,0:T(8,128)(2,1)S(1)} %pad_maximum_fusion.4), channel_id=1, source_target_pairs={{0,8},{1,9},{2,10},{3,11},{4,12},{5,13},{6,14},{7,15},{8,0},{9,1},... | collective-permute-start | bytes 589832 | tf_op jit(solution)/shard_map/ppermute | solution.py:583
  186.9 1.4 copy-start.4
  188.3 31.2 %all-to-all-start.4 = ((bf16[8,224,512]{2,1,0:T(8,128)(2,1)}), bf16[8,224,512]{2,1,0:T(8,128)(2,1)S(1)}, u32[]{:S(2)}, u32[]{:S(2)}) async-start(bf16[8,224,512]{2,1,0:T(8,128)(2,1)} %broadcast_in_dim.92), calls=%async_computation.4 | async-start | bytes 3670016 | tf_op jit(solution)/shard_map/all_to_all | solution.py:664
  196.3 1.7 copy-start.3
  228.1 1.8 copy-start

commit v3 on v2

--- a/solution.py
+++ b/solution.py
@@ -534,8 +534,8 @@
 
 
 def unpack(totals, *refs):
-    outs, (given, leave) = refs[:-2], refs[-2:]
-    rows = given.shape[1]
+    outs, (taken, given, arrive, leave) = refs[:-4], refs[-4:]
+    rows = taken.shape[1]
     width = totals.shape[2]
     edge_half, node_half = 2 * width, (totals.shape[1] - 2 * width) // rows * rows
     places = []
@@ -547,12 +547,20 @@
                     places.append((core, start + row, pair[0], goal))
                 else:
                     places.append((core, start + row, pair[1], goal - pair[0].shape[0]))
-    leaving = []
-    for n, (core, row, target, goal) in enumerate(places):
-        given[n] = totals[core, row : row + rows].astype(F32)
-        copy = pltpu.make_async_copy(given.at[n], target.at[pl.ds(goal, rows)], leave.at[n])
+    incoming = [
+        pltpu.make_async_copy(totals.at[core, pl.ds(row, rows)], taken.at[n], arrive.at[n])
+        for n, (core, row, _, _) in enumerate(places)
+    ]
+    leaving = [
+        pltpu.make_async_copy(given.at[n], goal.at[pl.ds(row, rows)], leave.at[n])
+        for n, (_, _, goal, row) in enumerate(places)
+    ]
+    for copy in incoming:
         copy.start()
-        leaving.append(copy)
+    for n in range(len(places)):
+        incoming[n].wait()
+        given[n] = taken[n].astype(F32)
+        leaving[n].start()
     for copy in leaving:
         copy.wait()
 
@@ -1019,13 +1027,15 @@
     parts = 7 * width // chunk
     weights = pl.pallas_call(
         unpack,
-        in_specs=[pl.BlockSpec(memory_space=pltpu.VMEM)],
+        in_specs=[unread()],
         out_specs=[unread()] * 4,
         out_shape=[
             jax.ShapeDtypeStruct((rows * width, width), F32) for rows in (3, 1, 2, 1)
         ],
         scratch_shapes=[
+            pltpu.VMEM((parts, chunk, width), BF16),
             pltpu.VMEM((parts, chunk, width), F32),
+            pltpu.SemaphoreType.DMA((parts,)),
             pltpu.SemaphoreType.DMA((parts,)),
         ],
         compiler_params=pltpu.CompilerParams(vmem_limit_bytes=VMEM),

time: 236 us -> 235 us (level)
  no operation moved by 1% of the time
where the time goes in v3:
time: 235 us
  Pallas kernels  151 us (64%)
  starting transfers between devices  35.6 us (15%)
  waiting for transfers between devices  14.3 us (6%)
  local copies, waits for them, and re-layouts  10.3 us (4%)
  other arithmetic  9.12 us (4%)
  blocking collectives  7.93 us (3%)
  matrix products  4.69 us (2%)
    pallas_call x1, Pallas kernels, shards(): pl.pallas_call(edge_backward, grid=(edges // short * pairs,), in_specs=[p...  49 us
    pallas_call x1, Pallas kernels, shards(): pl.pallas_call(edge_forward, grid=(edges // wide, samples), in_specs=[idx...  36.3 us
    pallas_call x1, Pallas kernels, shards(): pl.pallas_call(edge_start, grid=(edges // wide, samples), in_specs=[idx_b...  22.5 us
    pallas_call x1, Pallas kernels, shards(): pl.pallas_call(edge_gradient, grid=(edges // wide, samples), in_specs=[*t...  15.5 us
    pallas_call x1, Pallas kernels, shards(): pl.pallas_call(edge_outputs, grid=(edges // wide, samples), in_specs=[idx...  15.1 us
    all_to_all x2, starting transfers between devices, exchange(): swapped = lax.all_to_all(chunks, 'graph', 0, 0)  13.5 us
    all_to_all x2, starting transfers between devices, exchange_in_side(): lax.all_to_all(pieces, 'graph', 0, 0, axis_index_groups=side_groups())  13 us
    ppermute x3, waiting for transfers between devices, shift(): lax.ppermute(block, 'graph', [(i, (i + distance) % size) for i in range(s...  9.04 us
  transfers between devices with their start and end apart: 9, of which 4 were waited for; matrix products, arithmetic and copies ran while one was open for 6% of the time, Pallas kernels for 47%

profile of v3, /device:TPU:19, one launch (start us, length us, event | category | flops | bytes accessed | tf_op | source)
XLA Modules:
  0.0 234.5 jit_solution(10714042060376661324)
XLA Ops:
  2.1 3.5 %fusion.6 = bf16[768,512]{1,0:T(8,128)(2,1)} fusion(bf16[1280,512]{1,0:T(8,128)(2,1)} %bitcast.48, s32[768]{0:T(1024)S(1)} %add.126), kind=kOutput, calls=%fused_computation.10 | convolution fusion | flops 1008009216 | bytes 2100224 | tf_op jit(solution)/shard_map/dot_general | solution.py:19
  5.6 6.5 %all-to-all-start = ((bf16[16,48,512]{2,1,0:T(8,128)(2,1)}), bf16[16,48,512]{2,1,0:T(8,128)(2,1)S(1)}, u32[]{:S(2)}, u32[]{:S(2)}) async-start(bf16[16,48,512]{2,1,0:T(8,128)(2,1)} %bitcast.12), calls=%async_computation | async-start | bytes 1572864 | tf_op jit(solution)/shard_map/all_to_all | solution.py:603
  12.1 0.8 dynamic-slice_bitcast_fusion.1
  14.7 22.5 %edge_start.1.partial = bf16[4,2560,512]{2,1,0:T(8,128)(2,1)} custom-call(f32[2,8,1280]{2,1,0:T(8,128)} %bitcast.50, bf16[4,2560,512]{2,1,0:T(8,128)(2,1)} %x_high.1, bf16[4,320,512]{2,1,0:T(8,128)(2,1)} %nodes.3, bf16[1536,512]{1,0:T(8,128)(2,1)} %first.5, f32[8,512]{1,0:T(8,128)} %stack.55.vec), custom_call_target="tpu_custom_call" | custom-call | flops 16106127360 | bytes 20971520 | tf_op jit(solution)/shard_map/edge_start/pallas_call | solution.py:771
  37.8 1.0 broadcast_select_fusion.1.arrived
  38.8 36.3 %edge_forward.1 = (bf16[4,2560,512]{2,1,0:T(8,128)(2,1)}, bf16[4,2560,512]{2,1,0:T(8,128)(2,1)}, bf16[4,2560,512]{2,1,0:T(8,128)(2,1)}, f32[4,2560,128]{2,1,0:T(...) custom-call(f32[2,8,1280]{2,1,0:T(8,128)} %bitcast.51, ...), custom_call_target="tpu_custom_call" | custom-call | flops 21474836480 | bytes 41943040 | tf_op jit(solution)/shard_map/edge_forward/pallas_call | solution.py:797
  75.1 6.9 %all-to-all-start.1 = ((bf16[32,48,512]{2,1,0:T(8,128)(2,1)}), bf16[32,48,512]{2,1,0:T(8,128)(2,1)S(1)}, u32[]{:S(2)}, u32[]{:S(2)}) async-start(bf16[32,48,512]{2,1,0:T(8,128)(2,1)} %bitcast.47), calls=%async_computation.1 | async-start | bytes 3145728 | tf_op jit(solution)/shard_map/all_to_all | solution.py:649
  82.0 49.0 %edge_backward.1 = (bf16[4,2560,512]{2,1,0:T(8,128)(2,1)}, f32[4,8,512]{2,1,0:T(8,128)}, bf16[4,320,512]{2,1,0:T(8,128)(2,1)}, bf16[768,512]{1,0:T(8,128)(2,1)},...) custom-call(f32[5,8,512]{2,1,0:T(8,128)} %bitcast.52, ...), custom_call_target="tpu_custom_call" | custom-call | flops 37580963840 | bytes 52428800 | tf_op jit(solution)/shard_map/edge_backward/pallas_call | solution.py:874
  131.0 7.0 %all-to-all-start.2 = ((bf16[16,48,512]{2,1,0:T(8,128)(2,1)}), bf16[16,48,512]{2,1,0:T(8,128)(2,1)S(1)}, u32[]{:S(2)}, u32[]{:S(2)}) async-start(bf16[16,48,512]{2,1,0:T(8,128)(2,1)} %get-tuple-element.62.after), calls=%async_computation.2 | async-start | bytes 1572864 | tf_op jit(solution)/shard_map/all_to_all | solution.py:603
  138.0 8.6 %edge_totals.1 = (f32[4,320,512]{2,1,0:T(8,128)}, bf16[2048,512]{1,0:T(8,128)(2,1)}) custom-call(bf16[4,320,512]{2,1,0:T(8,128)(2,1)} %get-tuple-element.54.local, bf16[4,320,512]{2,1,0:T(8,128)(2,1)} %get-tuple-element.55.received, bf16[768,512]{1,0:T(8,128)(2,1)} %get-tuple-element.56.remote, ...), custom_call_target="tpu_custom_call", output_to_operand_aliasing={{1}: (7, {})} | custom-call | tf_op jit(solution)/shard_map/edge_totals/pallas_call | solution.py:944
  146.7 2.4 %constant_dynamic-slice_fusion = bf16[1024,512]{1,0:T(8,128)(2,1)} fusion(bf16[2048,512]{1,0:T(8,128)(2,1)} %get-tuple-element.63, s32[]{:T(128)S(6)} %select_n.100), kind=kLoop, calls=%fused_computation.71 | loop fusion | bytes 2097156 | tf_op jit(solution)/shard_map/dynamic_slice | solution.py:684
  149.1 0.9 collective-permute-start.1
  150.1 0.8 dynamic-slice_bitcast_fusion
  151.2 1.6 reduce_sum.50
  152.8 1.5 add_convert_fusion
  154.4 1.1 pad_maximum_fusion.1.after
  155.5 1.2 collective-permute-done.2
  156.7 0.9 all-to-all-done.2
  157.7 5.0 %all-to-all-start.3 = ((bf16[8,144,512]{2,1,0:T(8,128)(2,1)}), bf16[8,144,512]{2,1,0:T(8,128)(2,1)S(1)}, u32[]{:S(2)}, u32[]{:S(2)}) async-start(bf16[8,144,512]{2,1,0:T(8,128)(2,1)} %pad_maximum_fusion.1.after), calls=%async_computation.3 | async-start | bytes 2359296 | tf_op jit(solution)/shard_map/all_to_all | solution.py:672
  162.7 15.5 %edge_gradient.1 = bf16[4,2560,512]{2,1,0:T(8,128)(2,1)} custom-call(bf16[4,2560,512]{2,1,0:T(8,128)(2,1)} %cot_high.1, bf16[4,2560,512]{2,1,0:T(8,128)(2,1)} %cot_high.1, bf16[4,2560,512]{2,1,0:T(8,128)(2,1)} %get-tuple-element.68.hid_low.hid_high, bf16[4,2560,512]{2,1,0:T(8,128)(2,1)} %get-tuple-element.68.hid_low.hid_high, bf16[1536,512]{1,0:T(8,128)(2,1)} %first.5, ...), custom_call_target="tpu_custom_call" | custom-call | flops 5368709120 | bytes 31457280 | tf_op jit(solution)/shard_map/edge_gradient/pallas_call | solution.py:973
  178.5 0.7 collective-permute-start.3
  179.2 7.8 %collective-permute-done.3 = bf16[192,512]{1,0:T(8,128)(2,1)S(1)} collective-permute-done((bf16[192,512]{1,0:T(8,128)(2,1)S(1)}, bf16[192,512]{1,0:T(8,128)(2,1)S(1)}, u32[]{:S(2)}, u32[]{:S(2)}) %collective-permute-start.3) | collective-permute-done | bytes 196640 | tf_op jit(solution)/shard_map/ppermute | solution.py:591
  187.2 1.4 broadcast_in_dim.92
  188.6 8.0 %all-to-all-start.4 = ((bf16[8,224,512]{2,1,0:T(8,128)(2,1)}), bf16[8,224,512]{2,1,0:T(8,128)(2,1)S(1)}, u32[]{:S(2)}, u32[]{:S(2)}) async-start(bf16[8,224,512]{2,1,0:T(8,128)(2,1)} %broadcast_in_dim.92), calls=%async_computation.4 | async-start | bytes 3670016 | tf_op jit(solution)/shard_map/all_to_all | solution.py:672
  196.6 1.2 fusion.1
  198.3 2.1 add.133
  200.4 15.1 %edge_outputs.1 = bf16[4,2560,512]{2,1,0:T(8,128)(2,1)} custom-call(f32[2,8,1280]{2,1,0:T(8,128)} %bitcast.53, bf16[4,2560,512]{2,1,0:T(8,128)(2,1)} %x_high.1, bf16[4,2560,512]{2,1,0:T(8,128)(2,1)} %x_high.1, bf16[4,2560,512]{2,1,0:T(8,128)(2,1)} %get-tuple-element.51.nrm.nrm_low.nrm_high, bf16[4,2560,512]{2,1,0:T(8,128)(2,1)} %get-tuple-element.51.nrm.nrm_low.nrm_high, ...), custom_call_target="tpu_custom_call" | custom-call | bytes 31457280 | tf_op jit(solution)/shard_map/edge_outputs/pallas_call | solution.py:997
  215.5 4.4 %all-to-all-done.4 = bf16[8,224,512]{2,1,0:T(8,128)(2,1)S(1)} async-done(((bf16[8,224,512]{2,1,0:T(8,128)(2,1)}), bf16[8,224,512]{2,1,0:T(8,128)(2,1)S(1)}, u32[]{:S(2)}, u32[]{:S(2)}) %all-to-all-start.4) | async-done | bytes 1835040 | tf_op jit(solution)/shard_map/all_to_all | solution.py:672
  220.4 7.9 %all_to_all.30.totals = bf16[2,1808,512]{2,1,0:T(8,128)(2,1)S(1)} all-to-all(bf16[2,1808,512]{2,1,0:T(8,128)(2,1)S(1)} %broadcast_in_dim.93), channel_id=1, replica_groups=mesh['dp'=2,'graph'=16] {'dp'}, dimensions={0} | all-to-all | bytes 7405568 | tf_op jit(solution)/shard_map/all_to_all | solution.py:676
  228.4 0.7 fusion.22
  229.1 1.1 copy-done
  230.1 4.2 %unpack.1 = (f32[1536,512]{1,0:T(8,128)}, f32[512,512]{1,0:T(8,128)}, f32[1024,512]{1,0:T(8,128)}, f32[512,512]{1,0:T(8,128)}) custom-call(bf16[2,1808,512]{2,1,0:T(8,128)(2,1)} %copy-done), custom_call_target="tpu_custom_call" | custom-call | tf_op jit(solution)/shard_map/unpack/pallas_call | solution.py:1028
  (83 shorter events, 5.5 us)
Async XLA Ops:
  2.0 11.2 %copy-start.7 = (s32[2560]{0:T(1024)S(1)}, s32[2560]{0:T(1024)}, u32[]{:S(2)}) copy-start(s32[2560]{0:T(1024)} %param.38) | copy-start | bytes 30724
  2.0 11.2 %copy-start.8 = (s32[2560]{0:T(1024)S(1)}, s32[2560]{0:T(1024)}, u32[]{:S(2)}) copy-start(s32[2560]{0:T(1024)} %param.37) | copy-start | bytes 30724
  2.0 12.0 %copy-start.9 = (f32[512]{0:T(512)S(1)}, f32[512]{0:T(512)}, u32[]{:S(2)}) copy-start(f32[512]{0:T(512)} %param.23) | copy-start | bytes 6148
  2.0 11.9 %copy-start.10 = (f32[512]{0:T(512)S(1)}, f32[512]{0:T(512)}, u32[]{:S(2)}) copy-start(f32[512]{0:T(512)} %param.25) | copy-start | bytes 6148
  2.1 11.9 %copy-start.11 = (f32[512]{0:T(512)S(1)}, f32[512]{0:T(512)}, u32[]{:S(2)}) copy-start(f32[512]{0:T(512)} %param.26) | copy-start | bytes 6148
  2.1 11.9 %copy-start.12 = (f32[512]{0:T(512)S(1)}, f32[512]{0:T(512)}, u32[]{:S(2)}) copy-start(f32[512]{0:T(512)} %param.27) | copy-start | bytes 6148
  2.1 11.9 %copy-start.13 = (f32[512]{0:T(512)S(1)}, f32[512]{0:T(512)}, u32[]{:S(2)}) copy-start(f32[512]{0:T(512)} %param.29) | copy-start | bytes 6148
  2.1 11.9 %copy-start.14 = (f32[512]{0:T(512)S(1)}, f32[512]{0:T(512)}, u32[]{:S(2)}) copy-start(f32[512]{0:T(512)} %param.31) | copy-start | bytes 6148
  2.1 11.9 %copy-start.15 = (f32[512]{0:T(512)S(1)}, f32[512]{0:T(512)}, u32[]{:S(2)}) copy-start(f32[512]{0:T(512)} %param.32) | copy-start | bytes 6148
  2.1 11.9 %copy-start.16 = (f32[512]{0:T(512)S(1)}, f32[512]{0:T(512)}, u32[]{:S(2)}) copy-start(f32[512]{0:T(512)} %param.33) | copy-start | bytes 6148
  5.6 32.2 %all-to-all-start = ((bf16[16,48,512]{2,1,0:T(8,128)(2,1)}), bf16[16,48,512]{2,1,0:T(8,128)(2,1)S(1)}, u32[]{:S(2)}, u32[]{:S(2)}) async-start(bf16[16,48,512]{2,1,0:T(8,128)(2,1)} %bitcast.12), calls=%async_computation | async-start | bytes 1572864 | tf_op jit(solution)/shard_map/all_to_all | solution.py:603
  12.9 24.9 %collective-permute-start = (bf16[48,512]{1,0:T(8,128)(2,1)S(1)}, bf16[48,512]{1,0:T(8,128)(2,1)S(1)}, u32[]{:S(2)}, u32[]{:S(2)}) collective-permute-start(bf16[48,512]{1,0:T(8,128)(2,1)S(1)} %dynamic-slice_bitcast_fusion.1), channel_id=1, source_target_pairs={{0,8},{1,9},{2,10},{3,11},{4,12},{5,13},{6,14},{7,15},{8,0},{9,1},... | collective-permute-start | bytes 147464 | tf_op jit(solution)/shard_map/ppermute | solution.py:591
  14.7 22.5 %copy-start.17 = (s32[320]{0:T(512)S(1)}, s32[320]{0:T(512)}, u32[]{:S(2)}) copy-start(s32[320]{0:T(512)} %param.39) | copy-start | bytes 3844
  75.1 55.9 %all-to-all-start.1 = ((bf16[32,48,512]{2,1,0:T(8,128)(2,1)}), bf16[32,48,512]{2,1,0:T(8,128)(2,1)S(1)}, u32[]{:S(2)}, u32[]{:S(2)}) async-start(bf16[32,48,512]{2,1,0:T(8,128)(2,1)} %bitcast.47), calls=%async_computation.1 | async-start | bytes 3145728 | tf_op jit(solution)/shard_map/all_to_all | solution.py:649
  131.0 7.0 %copy-start.2 = (bf16[32,48,512]{2,1,0:T(8,128)(2,1)}, bf16[32,48,512]{2,1,0:T(8,128)(2,1)S(1)}, u32[]{:S(2)}) copy-start(bf16[32,48,512]{2,1,0:T(8,128)(2,1)S(1)} %all-to-all-done.1) | copy-start | bytes 4718596
  131.0 26.6 %all-to-all-start.2 = ((bf16[16,48,512]{2,1,0:T(8,128)(2,1)}), bf16[16,48,512]{2,1,0:T(8,128)(2,1)S(1)}, u32[]{:S(2)}, u32[]{:S(2)}) async-start(bf16[16,48,512]{2,1,0:T(8,128)(2,1)} %get-tuple-element.62.after), calls=%async_computation.2 | async-start | bytes 1572864 | tf_op jit(solution)/shard_map/all_to_all | solution.py:603
  138.0 12.0 %copy-start.5 = (f32[4,8,512]{2,1,0:T(8,128)S(1)}, f32[4,8,512]{2,1,0:T(8,128)}, u32[]{:S(2)}) copy-start(f32[4,8,512]{2,1,0:T(8,128)} %get-tuple-element.65) | copy-start | bytes 196612
  138.0 12.0 %copy-start.6 = (f32[4,8,512]{2,1,0:T(8,128)S(1)}, f32[4,8,512]{2,1,0:T(8,128)}, u32[]{:S(2)}) copy-start(f32[4,8,512]{2,1,0:T(8,128)} %get-tuple-element.64) | copy-start | bytes 196612
  146.7 6.2 %copy-start.1 = (bf16[2048,512]{1,0:T(8,128)(2,1)S(1)}, bf16[2048,512]{1,0:T(8,128)(2,1)}, u32[]{:S(2)}) copy-start(bf16[2048,512]{1,0:T(8,128)(2,1)} %get-tuple-element.63) | copy-start | bytes 6291460
  149.1 3.7 %collective-permute-start.1 = (bf16[1024,512]{1,0:T(8,128)(2,1)}, bf16[1024,512]{1,0:T(8,128)(2,1)}, u32[]{:S(2)}, u32[]{:S(2)}) collective-permute-start(bf16[1024,512]{1,0:T(8,128)(2,1)} %constant_dynamic-slice_fusion), channel_id=1, source_target_pairs={{0,16},{16,0},{1,17},{17,1},{2,18},{18,2},{3,19},{19,3},{4,20},{20... | collective-permute-start | bytes 3145736 | tf_op jit(solution)/shard_map/ppermute | solution.py:685
  150.9 5.8 %collective-permute-start.2 = (bf16[48,512]{1,0:T(8,128)(2,1)S(1)}, bf16[48,512]{1,0:T(8,128)(2,1)S(1)}, u32[]{:S(2)}, u32[]{:S(2)}) collective-permute-start(bf16[48,512]{1,0:T(8,128)(2,1)S(1)} %dynamic-slice_bitcast_fusion), channel_id=1, source_target_pairs={{0,8},{1,9},{2,10},{3,11},{4,12},{5,13},{6,14},{7,15},{8,0},{9,1},... | collective-permute-start | bytes 147464 | tf_op jit(solution)/shard_map/ppermute | solution.py:591
  157.7 20.5 %all-to-all-start.3 = ((bf16[8,144,512]{2,1,0:T(8,128)(2,1)}), bf16[8,144,512]{2,1,0:T(8,128)(2,1)S(1)}, u32[]{:S(2)}, u32[]{:S(2)}) async-start(bf16[8,144,512]{2,1,0:T(8,128)(2,1)} %pad_maximum_fusion.1.after), calls=%async_computation.3 | async-start | bytes 2359296 | tf_op jit(solution)/shard_map/all_to_all | solution.py:672
  178.5 8.6 %collective-permute-start.3 = (bf16[192,512]{1,0:T(8,128)(2,1)S(1)}, bf16[192,512]{1,0:T(8,128)(2,1)S(1)}, u32[]{:S(2)}, u32[]{:S(2)}) collective-permute-start(bf16[192,512]{1,0:T(8,128)(2,1)S(1)} %pad_maximum_fusion.4), channel_id=1, source_target_pairs={{0,8},{1,9},{2,10},{3,11},{4,12},{5,13},{6,14},{7,15},{8,0},{9,1},... | collective-permute-start | bytes 589832 | tf_op jit(solution)/shard_map/ppermute | solution.py:591
  187.2 1.4 copy-start.4
  188.6 31.2 %all-to-all-start.4 = ((bf16[8,224,512]{2,1,0:T(8,128)(2,1)}), bf16[8,224,512]{2,1,0:T(8,128)(2,1)S(1)}, u32[]{:S(2)}, u32[]{:S(2)}) async-start(bf16[8,224,512]{2,1,0:T(8,128)(2,1)} %broadcast_in_dim.92), calls=%async_computation.4 | async-start | bytes 3670016 | tf_op jit(solution)/shard_map/all_to_all | solution.py:672
  196.5 1.7 copy-start.3
  228.3 1.8 copy-start
